TPU v7x, 32 devices: a whole 2x2x4 slice. The times are simulated.
32 devices in a mesh: dp: 16 (over z, x, core), tensor: 2 (over y).
Axes of the slice: x: 2, y: 2, z: 4, core: 2. Of those that a mesh axis runs over, the one named last changes fastest.
Arguments:
- tokens: bfloat16 [32768, 1024], P(('dp', 'tensor')), may hold values from -6 to 6
- lengths: int32 [16, 4], P('dp'), may hold values from 1 to 1024, 2048 in all within a row
- cotangent: bfloat16 [32768, 1024], P(('dp', 'tensor')), may hold values from -6 to 6
- pre_gain: bfloat16 [1024], P(('dp', 'tensor')), may hold values from 0.099609375 to 1.8984375
- w_gate: bfloat16 [1024, 2048], P('dp', 'tensor'), may hold values from -0.1875 to 0.1875
- w_inner: bfloat16 [1024, 2048], P('dp', 'tensor'), may hold values from -0.1875 to 0.1875
- w_shared: bfloat16 [1024, 256], P(('dp', 'tensor')), may hold values from -0.1875 to 0.1875
- w_step: bfloat16 [1024, 32], P('dp', 'tensor'), may hold values from -0.1875 to 0.1875
- conv_inner: float32 [2048, 4], P('tensor'), may hold values from -3 to 3
- conv_inner_bias: float32 [2048], P('tensor'), may hold values from -0.5 to 0.5
- conv_shared: bfloat16 [256, 4], P(('dp', 'tensor')), may hold values from -3 to 3
- conv_shared_bias: bfloat16 [256], P(('dp', 'tensor')), may hold values from -0.5 to 0.5
- step_bias: float32 [32], P('tensor'), may hold values from -6 to -2
- decay_log: float32 [32], P('tensor'), may hold values from -4 to 1
- skip_gain: float32 [32], P('tensor'), may hold values from 0.5 to 1.5
- mix_gain: bfloat16 [2048], P('tensor'), may hold values from 0.099609375 to 1.8984375
- w_out: bfloat16 [2048, 1024], P('tensor', 'dp'), may hold values from -0.125 to 0.125
Outputs:
- output: bfloat16 [32768, 1024], P(('dp', 'tensor'))
- grad_tokens: float32 [32768, 1024], P(('dp', 'tensor'))
- grad_pre_gain: float32 [1024], P(('dp', 'tensor'))
- grad_w_gate: float32 [1024, 2048], P('dp', 'tensor')
- grad_w_inner: float32 [1024, 2048], P('dp', 'tensor')
- grad_w_shared: float32 [1024, 256], P(('dp', 'tensor'))
- grad_w_step: float32 [1024, 32], P('dp', 'tensor')
- grad_conv_inner: float32 [2048, 4], P('tensor')
- grad_conv_inner_bias: float32 [2048], P('tensor')
- grad_conv_shared: float32 [256, 4], P(('dp', 'tensor'))
- grad_conv_shared_bias: float32 [256], P(('dp', 'tensor'))
- grad_step_bias: float32 [32], P('tensor')
- grad_decay_log: float32 [32], P('tensor')
- grad_skip_gain: float32 [32], P('tensor')
- grad_mix_gain: float32 [2048], P('tensor')
- grad_w_out: float32 [2048, 1024], P('tensor', 'dp')
Inputs may be any that keep to these rules, and one draw needn't show every extreme that they name: `lengths`: each row sums to 2048, and its longest sequence has exactly 1024 tokens.
All inputs are finite; a program needn't handle non-finite values.
Results may differ from a plain program's by a relative error of at most 0.014.
Values may be sent and summed in bfloat16 or wider, within the bound.
A program may use at most 384 MiB of HBM per device.

v0:
```python
import math

import jax
import jax.numpy as jnp
from jax import lax
from jax.sharding import PartitionSpec as P

SCAN_BLOCK = 256


EPS = 1e-05
HIGH = lax.Precision.HIGHEST


def segment_ids(lengths, count):
    ends = jnp.cumsum(lengths)
    places = lax.broadcasted_iota(jnp.int32, (count, ends.shape[0]), 0)
    return jnp.sum((places >= ends[None, :]).astype(jnp.int32), axis=1)


def causal_conv(values, kernel, bias, seg):
    taps = kernel.shape[1]
    count = values.shape[0]
    padded = jnp.concatenate([jnp.zeros((taps - 1, values.shape[1]), values.dtype), values], axis=0)
    seg_pad = jnp.concatenate([jnp.full((taps - 1,), -1, jnp.int32), seg])
    total = jnp.zeros_like(values) + bias[None, :]
    for place in range(taps):
        keep = (seg_pad[place : place + count] == seg).astype(values.dtype)
        total = total + kernel[:, place][None, :] * padded[place : place + count] * keep[:, None]
    return total


def contract_last(left, right):
    return lax.dot_general(
        left, right, (((1,), (1,)), ((), ())), preferred_element_type=jnp.float32
    )


def contract_first(left, right):
    return lax.dot_general(
        left, right, (((0,), (0,)), ((), ())), preferred_element_type=jnp.float32
    )


def block_inner(pieces):
    c_part, b_part, x_part, step_part, logs_part, seg_part = pieces
    block = seg_part.shape[1]
    lower = lax.broadcasted_iota(jnp.int32, (block, block), 0) >= lax.broadcasted_iota(
        jnp.int32, (block, block), 1
    )
    same = (seg_part[:, :, None] == seg_part[:, None, :]) & lower[None]
    diff = logs_part[:, :, None, :] - logs_part[:, None, :, :]
    weights = jnp.exp(jnp.where(same[..., None], diff, -10000.0))
    scores = jnp.einsum("kin,kjn->kij", c_part, b_part, precision=HIGH)
    weighted = scores[..., None] * weights * step_part[:, None, :, :]
    return jnp.einsum("kijh,kjhp->kihp", weighted, x_part, precision=HIGH)


def blockwise_scan(xs, step, decay, bmat, cmat, seg, block):
    count, heads, width = xs.shape
    states = bmat.shape[1]
    blocks = count // block
    per = math.gcd(blocks, 4)
    outer = blocks // per
    x_k = xs.reshape(blocks, block, heads, width)
    step_k = step.reshape(blocks, block, heads)
    b_k = bmat.reshape(blocks, block, states)
    c_k = cmat.reshape(blocks, block, states)
    seg_k = seg.reshape(blocks, block)
    prev = jnp.concatenate([jnp.full((1,), -1, jnp.int32), seg_k[:-1, -1]])
    logs = jnp.cumsum(step_k * decay[None, None, :], axis=1)
    pieces = (
        c_k.reshape(outer, per, block, states),
        b_k.reshape(outer, per, block, states),
        x_k.reshape(outer, per, block, heads, width),
        step_k.reshape(outer, per, block, heads),
        logs.reshape(outer, per, block, heads),
        seg_k.reshape(outer, per, block),
    )
    inner = lax.map(jax.checkpoint(block_inner), pieces).reshape(blocks, block, heads, width)
    carried = (seg_k == prev[:, None]).astype(jnp.float32)[..., None] * jnp.exp(logs)
    tail = (
        jnp.exp(logs[:, -1:, :] - logs)
        * (seg_k == seg_k[:, -1:]).astype(jnp.float32)[..., None]
        * step_k
    )
    local = jnp.einsum("kjh,kjn,kjhp->khnp", tail, b_k, x_k, precision=HIGH)

    def carry_step(state, piece):
        factor, added = piece
        return (factor[:, None, None] * state + added, state)

    _, entering = lax.scan(
        carry_step, jnp.zeros((heads, states, width), jnp.float32), (carried[:, -1, :], local)
    )
    inner = inner + carried[..., None] * jnp.einsum("kin,khnp->kihp", c_k, entering, precision=HIGH)
    return inner.reshape(count, heads, width)


def shards(
    tokens,
    lengths,
    cotangent,
    pre_gain,
    w_gate,
    w_inner,
    w_shared,
    w_step,
    conv_inner,
    conv_inner_bias,
    conv_shared,
    conv_shared_bias,
    step_bias,
    decay_log,
    skip_gain,
    mix_gain,
    w_out,
):
    tensor_count = lax.axis_size("tensor")
    rows_dev, width = tokens.shape
    group = rows_dev * tensor_count
    local_heads = step_bias.shape[0]
    inner_local = w_gate.shape[1]
    head_width = inner_local // local_heads
    states = w_shared.shape[1] // 2
    inner_all = inner_local * tensor_count
    gate_full, inner_full, step_full, out_full = (
        lax.all_gather(w_gate, "dp", axis=0, tiled=True),
        lax.all_gather(w_inner, "dp", axis=0, tiled=True),
        lax.all_gather(w_step, "dp", axis=0, tiled=True),
        lax.all_gather(w_out, "dp", axis=1, tiled=True),
    )
    shared_full, gain_full, kernel_shared, bias_shared = (
        lax.all_gather(w_shared, ("dp", "tensor"), axis=0, tiled=True),
        lax.all_gather(pre_gain, ("dp", "tensor"), axis=0, tiled=True),
        lax.all_gather(conv_shared, ("dp", "tensor"), axis=0, tiled=True),
        lax.all_gather(conv_shared_bias, ("dp", "tensor"), axis=0, tiled=True),
    )
    rows = tokens.astype(jnp.float32)
    gain_pre = gain_full.astype(jnp.float32)[None, :]
    rinv = lax.rsqrt(jnp.mean(rows * rows, axis=-1, keepdims=True) + EPS)
    normed_in = (rows * rinv * gain_pre).astype(jnp.bfloat16)
    gathered = lax.all_gather(normed_in, "tensor", axis=0, tiled=True)
    gate = jnp.dot(gathered, gate_full, preferred_element_type=jnp.float32)
    inner_pre = jnp.dot(gathered, inner_full, preferred_element_type=jnp.float32)
    shared_pre = jnp.dot(gathered, shared_full, preferred_element_type=jnp.float32)
    step_raw = jnp.dot(gathered, step_full, preferred_element_type=jnp.float32)
    seg = segment_ids(lengths[0], group)

    def mixer(
        gate_in,
        inner_in,
        shared_in,
        step_in,
        kernel_inner,
        bias_inner,
        kernel_s,
        bias_s,
        step_b,
        decay_l,
        skip,
    ):
        inner_conv = jax.nn.silu(causal_conv(inner_in, kernel_inner, bias_inner, seg))
        shared_conv = jax.nn.silu(causal_conv(shared_in, kernel_s, bias_s, seg))
        step = jax.nn.softplus(step_in + step_b[None, :])
        decay = -jnp.exp(decay_l)
        heads_in = inner_conv.reshape(group, local_heads, head_width)
        scanned = blockwise_scan(
            heads_in, step, decay, shared_conv[:, :states], shared_conv[:, states:], seg, SCAN_BLOCK
        )
        scanned = scanned + skip[None, :, None] * heads_in
        return scanned.reshape(group, inner_local) * jax.nn.silu(gate_in)

    gated, mixer_back = jax.vjp(
        mixer,
        gate,
        inner_pre,
        shared_pre,
        step_raw,
        conv_inner,
        conv_inner_bias,
        kernel_shared.astype(jnp.float32),
        bias_shared.astype(jnp.float32),
        step_bias,
        decay_log,
        skip_gain,
    )
    square_sum = lax.psum(jnp.sum(gated * gated, axis=-1), "tensor")
    rmix = lax.rsqrt(square_sum / inner_all + EPS)[:, None]
    gain_mix = mix_gain.astype(jnp.float32)[None, :]
    mixed = (gated * rmix * gain_mix).astype(jnp.bfloat16)
    partial_value = jnp.dot(mixed, out_full, preferred_element_type=jnp.float32)
    out_rows = lax.psum_scatter(partial_value, "tensor", scatter_dimension=0, tiled=True)
    cot_all = lax.all_gather(cotangent, "tensor", axis=0, tiled=True)
    out_term = contract_first(mixed, cot_all)
    grad_mixed = contract_last(cot_all, out_full)
    gain_local = jnp.sum(grad_mixed * gated * rmix, axis=0)
    upstream = grad_mixed * gain_mix
    cross = lax.psum(jnp.sum(upstream * gated, axis=-1), "tensor")[:, None]
    grad_gated = upstream * rmix - gated * rmix**3 * cross / inner_all
    output = (rows + out_rows).astype(jnp.bfloat16)
    (
        d_gate,
        d_inner,
        d_shared,
        d_step,
        d_kernel_inner,
        d_bias_inner,
        d_kernel_shared,
        d_bias_shared,
        d_step_bias,
        d_decay,
        d_skip,
    ) = mixer_back(grad_gated)
    gate_low = d_gate.astype(jnp.bfloat16)
    inner_low = d_inner.astype(jnp.bfloat16)
    step_low = d_step.astype(jnp.bfloat16)
    grad_gate_w = contract_first(gathered, gate_low)
    grad_inner_w = contract_first(gathered, inner_low)
    grad_step_w = contract_first(gathered, step_low)
    back_part = (
        contract_last(gate_low, gate_full)
        + contract_last(inner_low, inner_full)
        + contract_last(step_low, step_full)
    )
    back_rows, shared_rows = (
        lax.psum_scatter(back_part, "tensor", scatter_dimension=0, tiled=True),
        lax.psum_scatter(d_shared, "tensor", scatter_dimension=0, tiled=True),
    )
    shared_low = shared_rows.astype(jnp.bfloat16)
    back_rows = back_rows + contract_last(shared_low, shared_full)
    grad_shared_w = contract_first(normed_in, shared_low)
    grad_pre = jnp.sum(back_rows * rows * rinv, axis=0)
    upstream_pre = back_rows * gain_pre
    grad_tokens = (
        upstream_pre * rinv
        - rows * rinv**3 * jnp.sum(upstream_pre * rows, axis=-1, keepdims=True) / width
        + cotangent.astype(jnp.float32)
    )
    owned_gate, owned_inner, owned_step, owned_out = (
        lax.psum_scatter(
            grad_gate_w.astype(jnp.bfloat16), "dp", scatter_dimension=0, tiled=True
        ).astype(jnp.float32),
        lax.psum_scatter(
            grad_inner_w.astype(jnp.bfloat16), "dp", scatter_dimension=0, tiled=True
        ).astype(jnp.float32),
        lax.psum_scatter(
            grad_step_w.astype(jnp.bfloat16), "dp", scatter_dimension=0, tiled=True
        ).astype(jnp.float32),
        lax.psum_scatter(
            out_term.astype(jnp.bfloat16), "dp", scatter_dimension=1, tiled=True
        ).astype(jnp.float32),
    )
    owned_shared, owned_pre, owned_kernel, owned_bias = (
        lax.psum_scatter(grad_shared_w, ("dp", "tensor"), scatter_dimension=0, tiled=True),
        lax.psum_scatter(grad_pre, ("dp", "tensor"), scatter_dimension=0, tiled=True),
        lax.psum_scatter(d_kernel_shared, ("dp", "tensor"), scatter_dimension=0, tiled=True),
        lax.psum_scatter(d_bias_shared, ("dp", "tensor"), scatter_dimension=0, tiled=True),
    )
    sum_kernel, sum_bias, sum_step, sum_decay, sum_skip, sum_gain = lax.psum(
        (d_kernel_inner, d_bias_inner, d_step_bias, d_decay, d_skip, gain_local), "dp"
    )
    return (
        output,
        grad_tokens,
        owned_pre,
        owned_gate,
        owned_inner,
        owned_shared,
        owned_step,
        sum_kernel,
        sum_bias,
        owned_kernel,
        owned_bias,
        sum_step,
        sum_decay,
        sum_skip,
        sum_gain,
        owned_out,
    )


def solution(mesh):
    in_specs = (
        P(("dp", "tensor"), None),
        P("dp", None),
        P(("dp", "tensor"), None),
        P(("dp", "tensor")),
        P("dp", "tensor"),
        P("dp", "tensor"),
        P(("dp", "tensor"), None),
        P("dp", "tensor"),
        P("tensor", None),
        P("tensor"),
        P(("dp", "tensor"), None),
        P(("dp", "tensor")),
        P("tensor"),
        P("tensor"),
        P("tensor"),
        P("tensor"),
        P("tensor", "dp"),
    )
    out_specs = (
        P(("dp", "tensor"), None),
        P(("dp", "tensor"), None),
        P(("dp", "tensor")),
        P("dp", "tensor"),
        P("dp", "tensor"),
        P(("dp", "tensor"), None),
        P("dp", "tensor"),
        P("tensor", None),
        P("tensor"),
        P(("dp", "tensor"), None),
        P(("dp", "tensor")),
        P("tensor"),
        P("tensor"),
        P("tensor"),
        P("tensor"),
        P("tensor", "dp"),
    )
    return jax.shard_map(shards, mesh=mesh, in_specs=in_specs, out_specs=out_specs, check_vma=False)
```

profile of v0, /device:TPU:0, one launch (start us, length us, event | category | flops | bytes accessed | tf_op | source)
XLA Modules:
  0.0 1489.5 jit_solution(10518213243670260886)
XLA Ops:
  9.0 42.0 %all-reduce.30 = (bf16[1024]{0:T(1024)(128)(2,1)S(1)}, bf16[256]{0:T(256)(128)(2,1)S(1)}) all-reduce(bf16[1024]{0:T(1024)(128)(2,1)S(1)} %dynamic-update-slice, bf16[256]{0:T(256)(128)(2,1)S(1)} %dynamic-update-slice.1), channel_id=1, replica_groups=mesh['dp'=16,'tensor'=2] {'dp','tensor'}, use_global_device_ids=true, to_apply=%add.23 | all-reduce | flops 1280 | bytes 5120
  63.9 65.9 %all-gather = bf16[32,8,4]{1,2,0:T(4,128)(2,1)S(1)} all-gather(bf16[1,8,4]{1,2,0:T(4,128)(2,1)S(1)} %bitcast.449), channel_id=1, replica_groups=mesh['dp'=16,'tensor'=2] {'dp','tensor'}, dimensions={0}, use_global_device_ids=true | all-gather | bytes 2112 | tf_op jit(solution)/shard_map/all_gather | solution.py:136
  130.2 17.5 %all-gather.1 = bf16[16,64,16]{1,2,0:T(8,128)(2,1)S(1)} all-gather(bf16[1,64,16]{1,2,0:T(8,128)(2,1)S(1)} %bitcast.448), channel_id=1, replica_groups=mesh['dp'=16,'tensor'=2] {'dp'}, dimensions={0}, use_global_device_ids=true | all-gather | bytes 34816 | tf_op jit(solution)/shard_map/all_gather | solution.py:130
  147.8 67.9 %all_gather.35 = bf16[1024,256]{1,0:T(8,128)(2,1)S(1)} all-gather(bf16[32,256]{1,0:T(8,128)(2,1)S(1)} %copy-done.67), channel_id=1, replica_groups=mesh['dp'=16,'tensor'=2] {'dp','tensor'}, dimensions={0}, use_global_device_ids=true | all-gather | bytes 540672 | tf_op jit(solution)/shard_map/all_gather | solution.py:134
  294.0 51.8 %while.70 = (s32[]{:T(128)}, f32[16,128,64]{2,1,0:T(8,128)S(1)}, f32[8,16,128,64]{3,2,1,0:T(8,128)}, f32[8,16,1,1]{1,3,2,0:T(1,128)}, f32[8,16]{1,0:T(8,128)}, /...) while((s32[]{:T(128)}, f32[16,128,64]{2,1,0:T(8,128)S(1)}, f32[8,16,128,64]{3,2,1,0:T(8,128)}, ...), condition=%wide.region_8.9_spmd.clone, body=%wide.region_7.8_spmd.clone.sunk | while | flops 524291 | bytes 5244216 | solution.py:93
  366.3 45.6 %while.69 = (s32[]{:T(128)}, f32[2,4,256,16,64]{2,4,3,1,0:T(8,128)}, f32[2,4,256,16,64]{2,4,3,1,0:T(8,128)}, f32[2,4,256,128]{3,2,1,0:T(8,128)S(1)}, f32[2,4,256...) while((s32[]{:T(128)}, ...), condition=%wide.region_6.7_spmd.clone, body=%wide.region_5.6_spmd.clone.sunk | while | flops 3641245696 | bytes 12662893 | solution.py:80
  367.8 21.4 %bitcast_dynamic-update-slice_fusion.15 = f32[2,4,256,16,64]{2,4,3,1,0:T(8,128)} fusion(f32[2,4,256,16,64]{2,4,3,1,0:T(8,128)} %get-tuple-element.1237, s32[]{:T(128)S(6)} %copy.358, f32[4,256,16]{1,2,0:T(8,128)S(1)} %get-tuple-element.1210, f32[4,256,16]{1,2,0:T(8,128)S(1)} %get-tuple-element.1211, f32[4,256,256]{2,1,0:T(8,128)S(1)} %fusion.232, ...), kind=kOutput, calls=%fused_computation.50.clone.1 | convolution fusion | flops 3238002688 | bytes 9896960 | tf_op jit(solution)/shard_map/jvp()/while/body/eval_jaxpr/kijh,kjhp->kihp/dot_general | solution.py:56
  390.5 21.4 %bitcast_dynamic-update-slice_fusion.15 = f32[2,4,256,16,64]{2,4,3,1,0:T(8,128)} fusion(f32[2,4,256,16,64]{2,4,3,1,0:T(8,128)} %get-tuple-element.1237, s32[]{:T(128)S(6)} %copy.358, f32[4,256,16]{1,2,0:T(8,128)S(1)} %get-tuple-element.1210, f32[4,256,16]{1,2,0:T(8,128)S(1)} %get-tuple-element.1211, f32[4,256,256]{2,1,0:T(8,128)S(1)} %fusion.232, ...), kind=kOutput, calls=%fused_computation.50.clone.1 | convolution fusion | flops 3238002688 | bytes 9896960 | tf_op jit(solution)/shard_map/jvp()/while/body/eval_jaxpr/kijh,kjhp->kihp/dot_general | solution.py:56
  504.6 20.9 %multiply_reduce_fusion.3 = (f32[1024]{0:T(1024)}, f32[2048,1024]{1,0:T(8,128)}, bf16[2048,1024]{1,0:T(8,128)(2,1)}) fusion(f32[2048,1024]{1,0:T(8,128)} %get-tuple-element.921, f32[2048,1024]{1,0:T(8,128)} %get-tuple-element.970, f32[2048]{0:T(1024)S(1)} %psum.57, f32[2048,1024]{1,0:T(8,128)} %get-tuple-element.917, f32[2048]{0:T(1024)S(1)} %get-tuple-element.955, ...), kind=kLoop, calls=%fused_computation.106 | loop fusion | flops 56622080 | bytes 54562816 | tf_op jit(solution)/shard_map/transpose(jvp())/reduce_sum | solution.py:171
  573.5 106.9 %while.68 = (s32[]{:T(128)}, f32[2,4,256,128]{3,2,1,0:T(8,128)}, f32[2,4,256,128]{3,2,1,0:T(8,128)}, f32[2,4,256,16,64]{2,4,3,1,0:T(8,128)}, f32[2,4,256,16]{2,3...) while((s32[]{:T(128)}, f32[2,4,256,128]{3,2,1,0:T(8,128)}, ...), condition=%wide.region_22.23_spmd, body=%wide.region_17.22_spmd.sunk | while | flops 7722024960 | bytes 122630504 | solution.py:80
  579.3 26.2 %fusion.225 = (f32[4,256,16]{1,2,0:T(8,128)S(1)}, f32[4,256,16]{1,2,0:T(8,128)S(1)}, f32[4,256,16]{1,2,0:T(8,128)S(1)}, f32[4,256,256]{2,1,0:T(8,128)S(1)}) fusion(f32[4,256,256]{2,1,0:T(8,128)S(1)} %fusion.224, f32[4,256,16]{1,2,0:T(8,128)S(1)} %get-tuple-element.1193, f32[4,256,16]{1,2,0:T(8,128)S(1)} %get-tuple-element.1194, ...), kind=kOutput, calls=%fused_computation.11.clone.1 | convolution fusion | flops 3275440128 | bytes 11075584 | tf_op jit(solution)/shard_map/transpose(jvp())/while/body/eval_jaxpr/checkpoint/kijh,kjhp->kihp/dot_general | solution.py:56
  632.6 26.2 %fusion.225 = (f32[4,256,16]{1,2,0:T(8,128)S(1)}, f32[4,256,16]{1,2,0:T(8,128)S(1)}, f32[4,256,16]{1,2,0:T(8,128)S(1)}, f32[4,256,256]{2,1,0:T(8,128)S(1)}) fusion(f32[4,256,256]{2,1,0:T(8,128)S(1)} %fusion.224, f32[4,256,16]{1,2,0:T(8,128)S(1)} %get-tuple-element.1193, f32[4,256,16]{1,2,0:T(8,128)S(1)} %get-tuple-element.1194, ...), kind=kOutput, calls=%fused_computation.11.clone.1 | convolution fusion | flops 3275440128 | bytes 11075584 | tf_op jit(solution)/shard_map/transpose(jvp())/while/body/eval_jaxpr/checkpoint/kijh,kjhp->kihp/dot_general | solution.py:56
  694.6 31.3 %fusion.105 = f32[8,256,128]{2,1,0:T(8,128)} fusion(f32[8,256,128]{2,1,0:T(8,128)S(1)} %bitcast.418, f32[8,16,128,64]{3,2,1,0:T(8,128)} %get-tuple-element.1326, f32[8,256,16,64]{1,3,2,0:T(8,128)} %copy.243, f32[8,256,16]{1,2,0:T(8,128)S(1)} %copy-done.24), kind=kOutput, calls=%fused_computation.179 | convolution fusion | flops 3223584768 | bytes 14811136 | tf_op jit(solution)/shard_map/transpose(jvp(kin,khnp->kihp))/dot_general | solution.py:96
  739.1 53.2 %while.71 = (s32[]{:T(128)}, f32[16,128,64]{2,1,0:T(8,128)S(1)}, f32[8,16]{1,0:T(8,128)S(1)}, f32[8,16,128,64]{3,2,1,0:T(8,128)}, f32[8,16,128,64]{2,3,1,0:T(8,1...) while((s32[]{:T(128)}, f32[16,128,64]{2,1,0:T(8,128)S(1)}, ...), condition=%wide.region_16.17_spmd.clone, body=%wide.region_14.16_spmd.clone.sunk | while | flops 786420 | bytes 5767704 | solution.py:93
  792.4 30.7 %fusion.102 = f32[8,256,128]{2,1,0:T(8,128)S(1)} fusion(f32[8,256,128]{2,1,0:T(8,128)} %bitcast.417, f32[8,16,128,64]{3,2,1,0:T(8,128)} %get-tuple-element.539, f32[8,256,16,64]{1,0,3,2:T(8,128)} %bitcast.396, f32[8,256,16]{1,2,0:T(8,128)S(1)} %copy-done.26), kind=kOutput, calls=%fused_computation.178 | convolution fusion | flops 3223584768 | bytes 14811136 | tf_op jit(solution)/shard_map/transpose(jvp(kjh,kjn,kjhp->khnp))/dot_general | solution.py:87
  829.4 19.6 %bitcast_add_fusion.2 = (f32[8,256,16,64]{1,3,2,0:T(8,128)}, f32[8,256,16,64]{1,3,2,0:T(8,128)S(1)}) fusion(f32[2,4,256,16,64]{2,4,3,1,0:T(8,128)} %get-tuple-element.540, f32[8,256,16]{1,2,0:T(8,128)S(1)} %copy-done.26, f32[8,256,128,1]{2,1,3,0:T(8,128)S(1)} %bitcast.402, f32[8,16,128,64]{3,2,1,0:T(8,128)} %get-tuple-element.539), kind=kOutput, calls=%fused_computation.97 | convolution fusion | flops 3225419776 | bytes 30539776 | tf_op jit(solution)/shard_map/transpose(jvp(kjh,kjn,kjhp->khnp))/dot_general | solution.py:87
  869.7 19.9 %reduce-window.31 = f32[8,16,2,128]{3,1,2,0:T(8,128)S(1)} reduce-window(f32[8,16,2,128]{3,1,2,0:T(8,128)S(1)} %copy_bitcast_fusion.1, f32[]{:T(128)} %constant.191.clone.1), window={size=1x1x1x128 pad=0_0x0_0x0_0x0_127}, to_apply=%region_25.26 | reduce-window | flops 4161536 | bytes 262148 | tf_op jit(solution)/shard_map/reduce-window.3
  943.9 24.5 %multiply_reduce_fusion.7 = (f32[1024]{0:T(1024)S(1)}, f32[1024]{0:T(1024)S(1)}, f32[1024]{0:T(1024)S(1)}, f32[1024]{0:T(1024)S(1)}, f32[1024]{0:T(1024)S(1)}, /*index=5*/f32[2048,1024]{1,0:T(8,128)S(1)}) fusion(f32[2048,1024]{1,0:T(8,128)} %copy-done.4, f32[2048]{0:T(1024)S(1)} %copy-done.33, f32[2048]{0:T(1024)S(1)} %copy-done.36, ...), kind=kLoop, calls=%fused_computation.110 | loop fusion | flops 48229376 | bytes 41992192 | tf_op jit(solution)/shard_map/transpose(jvp())/reduce_sum | solution.py:29
  1034.8 58.4 %all-reduce.29 = (f32[1024,4]{0,1:T(4,128)}, f32[1024]{0:T(1024)}, f32[16]{0:T(128)}, f32[16]{0:T(128)}, f32[16]{0:T(128)}, /*index=5*/f32[1024]{0:T(1024)}) all-reduce(f32[1024,4]{0,1:T(4,128)S(1)} %pad_add_fusion.6, f32[1024]{0:T(1024)S(1)} %get-tuple-element.823, ...), channel_id=1, replica_groups=mesh['dp'=16,'tensor'=2] {'dp'}, use_global_device_ids=true, to_apply=%region_40.41 | all-reduce | flops 6192 | bytes 49536 | tf_op jit(solution)/shard_map/psum | solution.py:260
  1097.9 43.4 %reduce-scatter.20.cloned.1.call-done = bf16[64,1024]{1,0:T(8,128)(2,1)} async-done(((bf16[1024,1024]{1,0:T(8,128)(2,1)}), bf16[64,1024]{1,0:T(8,128)(2,1)}) %reduce-scatter.20.cloned.1.call-update) | async-done | bytes 131088 | tf_op jit(solution)/shard_map/reduce_scatter | solution.py:244
  1142.9 99.0 %reduce-scatter.14.cloned.1.call-done = f32[1024,1024]{1,0:T(8,128)} async-done(((f32[2048,1024]{1,0:T(8,128)}), f32[1024,1024]{1,0:T(8,128)}) %reduce-scatter.14.cloned.1.call-update) | async-done | bytes 4194320 | tf_op jit(solution)/shard_map/reduce_scatter | solution.py:227
  1247.9 40.1 %all-reduce.28 = (f32[1024]{0:T(1024)S(1)}, f32[256,4]{0,1:T(4,128)S(1)}, f32[256]{0:T(256)S(1)}) all-reduce(f32[1024]{0:T(1024)S(1)} %get-tuple-element.824, f32[256,4]{0,1:T(4,128)S(1)} %pad_add_fusion.7, f32[256]{0:T(256)S(1)} %get-tuple-element.830), channel_id=5, replica_groups=mesh['dp'=16,'tensor'=2] {'dp','tensor'}, use_global_device_ids=true, to_apply=%region_31.32.clone | all-reduce | flops 2304 | bytes 18432
  1289.8 55.1 %reduce-scatter.12.cloned.1.call-done = f32[1024,1024]{1,0:T(8,128)} async-done(((f32[2048,1024]{1,0:T(8,128)}), f32[1024,1024]{1,0:T(8,128)}) %reduce-scatter.12.cloned.1.call-update) | async-done | bytes 4194320 | tf_op jit(solution)/shard_map/reduce_scatter | solution.py:193
  1351.4 131.0 %reduce-scatter.22.cloned.1.call-done = f32[32,256]{1,0:T(8,128)} async-done(((f32[1024,256]{1,0:T(8,128)}), f32[32,256]{1,0:T(8,128)}) %reduce-scatter.22.cloned.1.call-update) | async-done | bytes 32784 | tf_op jit(solution)/shard_map/reduce_scatter | solution.py:255
  (497 shorter events, 610.0 us)
Async XLA Ops:
  7.3 208.7 %copy-start.82 = (f32[16]{0:T(128)S(1)}, f32[16]{0:T(128)}, u32[]{:S(2)}) copy-start(f32[16]{0:T(128)} %param.37) | copy-start | bytes 196
  7.3 208.6 %all-gather.8.cloned.1.call-start = ((), (), s32[]{:S(2)}) async-start(), calls=%async_computation.8 | async-start | bytes 6291456 | tf_op jit(solution)/shard_map/all_gather | solution.py:143
  57.8 176.7 %all-gather.10.cloned.1.call-start = ((), (), s32[]{:S(2)}) async-start(), calls=%async_computation.9 | async-start | bytes 2228224 | tf_op jit(solution)/shard_map/all_gather | solution.py:129
  58.6 405.2 %all-gather.12.cloned.1.call-start = ((), (), s32[]{:S(2)}) async-start(), calls=%async_computation.10 | async-start | bytes 2228224 | tf_op jit(solution)/shard_map/all_gather | solution.py:128
  59.3 425.7 %all-gather.14.cloned.1.call-start = ((), (), s32[]{:S(2)}) async-start(), calls=%async_computation.11 | async-start | bytes 2228224 | tf_op jit(solution)/shard_map/all_gather | solution.py:131
  59.9 425.1 %all-gather.16.cloned.1.call-start = ((), (), s32[]{:S(2)}) async-start(), calls=%async_computation.13 | async-start | bytes 6291456 | tf_op jit(solution)/shard_map/all_gather | solution.py:194
  60.5 970.2 %reduce-scatter.16.cloned.1.call-start = ((), (), s32[]{:S(2)}) async-start(), calls=%async_computation.15 | async-start | bytes 3145728 | tf_op jit(solution)/shard_map/reduce_scatter | solution.py:228
  61.9 168.3 %copy-start.34 = (f32[2048]{0:T(1024)}, f32[2048]{0:T(1024)S(1)}, u32[]{:S(2)}) copy-start(f32[2048]{0:T(1024)S(1)} %get-tuple-element.961) | copy-start | bytes 24580
  61.9 179.6 %copy-start.30 = (f32[2048]{0:T(1024)}, f32[2048]{0:T(1024)S(1)}, u32[]{:S(2)}) copy-start(f32[2048]{0:T(1024)S(1)} %get-tuple-element.959) | copy-start | bytes 24580
  61.9 179.6 %copy-start.32 = (f32[2048]{0:T(1024)}, f32[2048]{0:T(1024)S(1)}, u32[]{:S(2)}) copy-start(f32[2048]{0:T(1024)S(1)} %get-tuple-element.960) | copy-start | bytes 24580
  61.9 158.2 %copy-start.83 = (f32[16]{0:T(128)}, f32[16]{0:T(128)S(1)}, u32[]{:S(2)}) copy-start(f32[16]{0:T(128)S(1)} %exponential_negate_fusion) | copy-start | bytes 196
  225.8 196.6 %copy-start.23 = (f32[8,256,16]{1,2,0:T(8,128)}, f32[8,256,16]{1,2,0:T(8,128)S(1)}, u32[]{:S(2)}) copy-start(f32[8,256,16]{1,2,0:T(8,128)S(1)} %get-tuple-element.948) | copy-start | bytes 393220
  829.4 263.9 %reduce-scatter.26.cloned.1.call-start = ((), (), s32[]{:S(2)}) async-start(), calls=%async_computation.20 | async-start | bytes 278528
  894.2 200.4 %reduce-scatter.24.cloned.1.call-start = ((), (), s32[]{:S(2)}) async-start(), calls=%async_computation.19 | async-start | bytes 2228224 | tf_op jit(solution)/shard_map/reduce_scatter | solution.py:250
  905.2 191.1 %reduce-scatter.18.cloned.1.call-start = ((), (), s32[]{:S(2)}) async-start(), calls=%async_computation.16 | async-start | bytes 2228224 | tf_op jit(solution)/shard_map/reduce_scatter | solution.py:241
  943.8 197.5 %reduce-scatter.20.cloned.1.call-start = ((), (), s32[]{:S(2)}) async-start(), calls=%async_computation.17 | async-start | bytes 2228224 | tf_op jit(solution)/shard_map/reduce_scatter | solution.py:244
  1001.6 240.4 %reduce-scatter.14.cloned.1.call-start = ((), (), s32[]{:S(2)}) async-start(), calls=%async_computation.14 | async-start | bytes 12582912 | tf_op jit(solution)/shard_map/reduce_scatter | solution.py:227
  1018.4 326.4 %reduce-scatter.12.cloned.1.call-start = ((), (), s32[]{:S(2)}) async-start(), calls=%async_computation.12 | async-start | bytes 12582912 | tf_op jit(solution)/shard_map/reduce_scatter | solution.py:193
  1030.5 211.4 %copy-start.6 = (bf16[1024,1024]{1,0:T(8,128)(2,1)S(1)}, bf16[1024,1024]{1,0:T(8,128)(2,1)}, u32[]{:S(2)}) copy-start(bf16[1024,1024]{1,0:T(8,128)(2,1)} %param.25) | copy-start | bytes 6291460
  1030.5 211.4 %copy-start.28 = (bf16[1024,256]{1,0:T(8,128)(2,1)S(1)}, bf16[1024,256]{1,0:T(8,128)(2,1)}, u32[]{:S(2)}) copy-start(bf16[1024,256]{1,0:T(8,128)(2,1)} %copy-done.27) | copy-start | bytes 1572868
  1030.5 211.4 %copy-start.49 = (f32[1024]{0:T(1024)S(1)}, f32[1024]{0:T(1024)}, u32[]{:S(2)}) copy-start(f32[1024]{0:T(1024)} %copy-done.48) | copy-start | bytes 12292
  1030.6 211.4 %copy-start.51 = (f32[1024]{0:T(1024)S(1)}, f32[1024]{0:T(1024)}, u32[]{:S(2)}) copy-start(f32[1024]{0:T(1024)} %copy-done.50) | copy-start | bytes 12292
  1030.6 451.9 %reduce-scatter.22.cloned.1.call-start = ((), (), s32[]{:S(2)}) async-start(), calls=%async_computation.18 | async-start | bytes 1081344 | tf_op jit(solution)/shard_map/reduce_scatter | solution.py:255
  1034.5 310.4 %copy-start.69 = (f32[1024]{0:T(1024)S(1)}, f32[1024]{0:T(1024)}, u32[]{:S(2)}) copy-start(f32[1024]{0:T(1024)} %get-tuple-element.962) | copy-start | bytes 12292
  (91 other events, 2387.4 us)
Sparse Core Ops, SparseCore 0:
  57.9 57.0 all-gather.7
  117.2 41.3 all-gather.9
  160.8 40.4 all-gather.11
  203.3 40.4 all-gather.13
  245.1 55.5 all-gather.15
  829.5 29.3 reduce-scatter.15
  894.3 52.7 reduce-scatter.25
  951.4 60.5 reduce-scatter.23
  1015.7 60.9 reduce-scatter.17
  1080.7 60.5 reduce-scatter.19
  1143.6 98.2 reduce-scatter.13
  1244.2 100.6 reduce-scatter.11
  1347.7 134.7 reduce-scatter.21
where the time goes:
time: 1500 us; the launch traced here: 1490 us
  matrix products  357 us (24%)
  waiting for transfers between devices  331 us (22%)
  blocking collectives  302 us (20%)
  local copies, waits for them, and re-layouts  281 us (19%)
  other arithmetic  200 us (13%)
  between operations  15.8 us (1%)
    reduce_scatter x1, waiting for transfers between devices, shards(): lax.psum_scatter(grad_shared_w, ('dp', 'tensor'), scatter_dimension=0, ti...  131 us
    dot_general x6, matrix products, block_inner(): return jnp.einsum('kijh,kjhp->kihp', weighted, x_part, precision=HIGH)  124 us
    reduce_scatter x1, waiting for transfers between devices, shards(): lax.psum_scatter(back_part, 'tensor', scatter_dimension=0, tiled=True)  99 us
    unnamed x2, blocking collectives  82.1 us
    all_gather x1, blocking collectives, shards(): lax.all_gather(w_shared, ('dp', 'tensor'), axis=0, tiled=True)  67.9 us
    all_gather x1, blocking collectives, shards(): lax.all_gather(conv_shared, ('dp', 'tensor'), axis=0, tiled=True)  65.9 us
    dot_general x3, matrix products, blockwise_scan(): local = jnp.einsum('kjh,kjn,kjhp->khnp', tail, b_k, x_k, precision=HIGH)  60.8 us
    psum x1, blocking collectives, shards(): lax.psum((d_kernel_inner, d_bias_inner, d_step_bias, d_decay, d_skip, gai...  58.4 us
  transfers between devices with their start and end apart: 13, of which 4 were waited for; matrix products, arithmetic and copies ran while one was open for 33% of the time, Pallas kernels for 0%

commit v1 on v0

v1 whole, which is shorter than its diff:
```python
import functools

import jax
import jax.numpy as jnp
from jax import lax
from jax.experimental import pallas as pl
from jax.experimental.pallas import tpu as pltpu
from jax.sharding import PartitionSpec as P

EPS = 1e-05
HIGH = lax.Precision.HIGHEST
Q = 128
LANES = 128
F32 = jnp.float32
BF16 = jnp.bfloat16
LAST = (((1,), (1,)), ((), ()))
FIRST = (((0,), (0,)), ((), ()))
VMEM_LIMIT = 56 * 1024 * 1024


def segment_ids(lengths, count):
    ends = jnp.cumsum(lengths)
    places = lax.broadcasted_iota(jnp.int32, (count, ends.shape[0]), 0)
    return jnp.sum((places >= ends[None, :]).astype(jnp.int32), axis=1)


def contract_last(left, right):
    return lax.dot_general(left, right, LAST, preferred_element_type=F32)


def contract_first(left, right):
    return lax.dot_general(left, right, FIRST, preferred_element_type=F32)


def mul(left, right):
    return jnp.dot(left, right, preferred_element_type=F32)


def halves(value):
    high = value.astype(BF16)
    return high, (value - high.astype(F32)).astype(BF16)


def spread(value, expand):
    high, low = halves(value)
    return mul(high, expand) + mul(low, expand)


def per_head(value, expand):
    high, low = halves(value)
    return contract_last(high, expand) + contract_last(low, expand)


def shifted(value, halo, cols):
    ext = jnp.concatenate([halo, value], axis=0)
    return [pltpu.roll(ext, s, axis=0)[8:] * cols[:, s : s + 1] for s in (1, 2, 3)]


def convolve(value, earlier, taps):
    total = taps[4:5] + taps[3:4] * value
    for s in (1, 2, 3):
        total = total + taps[3 - s : 4 - s] * earlier[s - 1]
    return total


def convolve_back(grad, later, cols, taps):
    ext = jnp.concatenate([grad, later], axis=0)
    count = grad.shape[0]
    total = taps[3:4] * grad
    for s in (1, 2, 3):
        moved = pltpu.roll(ext, count + 8 - s, axis=0)[:count]
        total = total + taps[3 - s : 4 - s] * (moved * cols[:, 5 + s : 6 + s])
    return total


def tap_grads(grad, value, earlier):
    rows = [jnp.sum(grad * earlier[2 - k], axis=0, keepdims=True) for k in range(3)]
    rows.append(jnp.sum(grad * value, axis=0, keepdims=True))
    rows.append(jnp.sum(grad, axis=0, keepdims=True))
    return rows


def block_terms(pre_ref, halo_ref, sh_ref, halo_sh_ref, step_ref, rate_ref, rate_row_ref, cols, seg_row_ref, ti, ts, expand):
    pre, sh = pre_ref[...], sh_ref[...]
    near, near_s = shifted(pre, halo_ref[...], cols), shifted(sh, halo_sh_ref[...], cols)
    z, zs = convolve(pre, near, ti), convolve(sh, near_s, ts)
    rows = lax.broadcasted_iota(jnp.int32, (Q, Q), 0)
    lanes = lax.broadcasted_iota(jnp.int32, (Q, Q), 1)
    lower = (rows >= lanes).astype(F32)
    upper = (rows <= lanes).astype(F32)
    logs = jnp.dot(lower, rate_ref[...], precision=HIGH, preferred_element_type=F32)
    logs_row = jnp.dot(rate_row_ref[...], upper, precision=HIGH, preferred_element_type=F32)
    step_e = spread(step_ref[...], expand)
    carried = spread(jnp.exp(logs) * cols[:, 4:5], expand)
    tail = spread(jnp.exp(logs[Q - 1 : Q] - logs) * cols[:, 5:6], expand)
    mask = (cols[:, 0:1] == seg_row_ref[0:1, :]) & (rows >= lanes)
    return pre, sh, near, near_s, z, zs, logs, logs_row, step_e, carried, tail, mask


def decays(logs, logs_row, mask, h):
    diff = logs[:, h : h + 1] - logs_row[h : h + 1, :]
    return jnp.exp(jnp.where(mask, diff, -10000.0))


def forward_kernel(
    heads, pre_ref, halo_ref, gate_ref, sh_ref, halo_sh_ref, step_ref, rate_ref, rate_row_ref,
    cols_ref, seg_row_ref, ti_ref, ts_ref, expand_ref, gated_ref, states_ref, sums_ref, state,
):
    @pl.when(pl.program_id(0) == 0)
    def _():
        state[...] = jnp.zeros_like(state)

    cols, ti, ts, expand = cols_ref[...], ti_ref[...], ts_ref[...], expand_ref[...]
    _, _, _, _, z, zs, logs, logs_row, step_e, carried, tail, mask = block_terms(
        pre_ref, halo_ref, sh_ref, halo_sh_ref, step_ref, rate_ref, rate_row_ref, cols, seg_row_ref, ti, ts, expand
    )
    x = z * jax.nn.sigmoid(z)
    shared = (zs * jax.nn.sigmoid(zs)).astype(BF16)
    b, c = shared[:, :LANES], shared[:, LANES:]
    xs = step_e * x
    low_lanes = ti[7:8]
    x_even = (xs * low_lanes).astype(BF16)
    x_odd = (xs * (1.0 - low_lanes)).astype(BF16)
    entering = state[...]
    entering_low = entering.astype(BF16)
    states_ref[...] = entering_low
    scores = contract_last(c, b)
    base = carried * mul(c, entering_low) + ti[5:6] * x
    state[...] = carried[Q - 1 : Q] * entering + contract_first(b, (tail * xs).astype(BF16))
    total = jnp.zeros((Q, LANES), F32)
    for pair in range(heads // 2):
        at = slice(pair * LANES, (pair + 1) * LANES)
        both = jnp.concatenate(
            [scores * decays(logs, logs_row, mask, 2 * pair + i) for i in range(2)], axis=1
        ).astype(BF16)
        y = base[:, at] + mul(both, jnp.concatenate([x_even[:, at], x_odd[:, at]], axis=0))
        gate = gate_ref[:, at]
        gated = y * (gate * jax.nn.sigmoid(gate))
        gated_ref[:, at] = gated
        total = total + gated * gated
    sums_ref[...] = jnp.broadcast_to(jnp.sum(total, axis=1, keepdims=True), (Q, LANES))


def backward_kernel(
    heads, pre_ref, halo_ref, gate_ref, sh_ref, halo_sh_ref, step_ref, rate_ref, rate_row_ref,
    cols_ref, seg_row_ref, ti_ref, ts_ref, expand_ref, states_ref, gm_ref, gated_ref, norms_ref,
    low_ref, dsh_ref, dstep_ref, dlog_ref, dlog_row_ref, acc_i_ref, acc_s_ref,
    dstate, later, later_s,
):
    @pl.when(pl.program_id(0) == 0)
    def _():
        dstate[...] = jnp.zeros_like(dstate)
        later[...] = jnp.zeros_like(later)
        later_s[...] = jnp.zeros_like(later_s)
        acc_i_ref[...] = jnp.zeros_like(acc_i_ref)
        acc_s_ref[...] = jnp.zeros_like(acc_s_ref)

    width = pre_ref.shape[1]
    cols, ti, ts, expand = cols_ref[...], ti_ref[...], ts_ref[...], expand_ref[...]
    pre, sh, near, near_s, z, zs, logs, logs_row, step_e, carried, tail, mask = block_terms(
        pre_ref, halo_ref, sh_ref, halo_sh_ref, step_ref, rate_ref, rate_row_ref, cols, seg_row_ref, ti, ts, expand
    )
    sig, sig_s = jax.nn.sigmoid(z), jax.nn.sigmoid(zs)
    x = z * sig
    shared = (zs * sig_s).astype(BF16)
    b, c = shared[:, :LANES], shared[:, LANES:]
    xs = step_e * x
    low_lanes = ti[7:8]
    high_lanes = 1.0 - low_lanes
    x_low = xs.astype(BF16)
    x_even = (xs * low_lanes).astype(BF16)
    x_odd = (xs * high_lanes).astype(BF16)
    skip = ti[5:6]

    gm, gated, gate, norms = gm_ref[...], gated_ref[...], gate_ref[...], norms_ref[...]
    rmix, pull = norms[:, 0:1], norms[:, 1:2]
    dgated = gm * ti[6:7] * rmix - gated * pull
    dgain = jnp.sum(gm * gated * rmix, axis=0, keepdims=True)
    sig_g = jax.nn.sigmoid(gate)
    dy = dgated * (gate * sig_g)
    dgate_scale = dgated * (sig_g * (1.0 + gate * (1.0 - sig_g)))
    dy_even = (dy * low_lanes).astype(BF16)
    dy_odd = (dy * high_lanes).astype(BF16)

    entering = states_ref[...]
    leaving = dstate[...]
    leaving_low = leaving.astype(BF16)
    scores = contract_last(c, b)
    from_state = carried * mul(c, entering)
    base = from_state + skip * x
    carried_dy = carried * dy
    carried_low = carried_dy.astype(BF16)
    tail_x = tail * xs
    tail_low = tail_x.astype(BF16)
    reach = mul(b, leaving_low)
    last_row = carried[Q - 1 : Q]
    pulled = jnp.sum(entering.astype(F32) * leaving, axis=0, keepdims=True) * last_row
    dstate[...] = last_row * leaving + contract_first(c, carried_low)

    lane = lax.broadcasted_iota(jnp.int32, (Q, LANES), 1)
    dscores = jnp.zeros((Q, Q), F32)
    row_sums = jnp.zeros((Q, LANES), F32)
    col_sums = []
    grads = []
    for pair in range(heads // 2):
        at = slice(pair * LANES, (pair + 1) * LANES)
        weights = [decays(logs, logs_row, mask, 2 * pair + i) for i in range(2)]
        mats = [(scores * w).astype(BF16) for w in weights]
        y = base[:, at] + mul(
            jnp.concatenate(mats, axis=1), jnp.concatenate([x_even[:, at], x_odd[:, at]], axis=0)
        )
        low_ref[:, at] = (dgate_scale[:, at] * y).astype(BF16)
        dys = jnp.concatenate([dy_even[:, at], dy_odd[:, at]], axis=0)
        cross = contract_last(dys, x_low[:, at])
        for i in range(2):
            part = cross[i * Q : (i + 1) * Q] * weights[i]
            dscores = dscores + part
            part = part * scores
            h = 2 * pair + i
            row_sums = jnp.where(lane == h, jnp.sum(part, axis=1, keepdims=True), row_sums)
            col_sums.append(jnp.sum(part, axis=0, keepdims=True))
        grads.append(contract_first(jnp.concatenate(mats, axis=0), dys))
    spare = dlog_row_ref.shape[0] - heads
    if spare:
        col_sums.append(jnp.zeros((spare, Q), F32))
    dlog_row_ref[...] = jnp.concatenate(col_sums, axis=0)
    dxs = jnp.concatenate(grads, axis=1) + tail * reach

    tail_term = tail_x * reach
    at_end = pulled + jnp.sum(tail_term, axis=0, keepdims=True)
    ends = lax.broadcasted_iota(jnp.int32, (Q, width), 0) == Q - 1
    log_term = dy * from_state - tail_term + jnp.where(ends, at_end, 0.0)
    dlog_ref[...] = row_sums + per_head(log_term, expand)
    dstep_ref[...] = per_head(x * dxs, expand)

    dx = step_e * dxs + skip * dy
    dz = dx * (sig * (1.0 + z * (1.0 - sig)))
    low_ref[:, width:] = convolve_back(dz, later[...], cols, ti).astype(BF16)
    later[...] = dz[:8]
    rows = tap_grads(dz, pre, near)
    rows += [jnp.sum(dy * x, axis=0, keepdims=True), dgain, jnp.zeros((1, width), F32)]
    acc_i_ref[...] += jnp.concatenate(rows, axis=0)

    dlow = dscores.astype(BF16)
    dc = mul(dlow, b) + contract_last(carried_low, entering)
    db = contract_first(dlow, c) + contract_last(tail_low, leaving_low)
    dzs = jnp.concatenate([db, dc], axis=1) * (sig_s * (1.0 + zs * (1.0 - sig_s)))
    dsh_ref[...] = convolve_back(dzs, later_s[...], cols, ts)
    later_s[...] = dzs[:8]
    rows = tap_grads(dzs, sh, near_s) + [jnp.zeros((3, dzs.shape[1]), F32)]
    acc_s_ref[...] += jnp.concatenate(rows, axis=0)


def block_specs(width, shared_width, row_heads, blocks, place):
    def halo(k):
        return jnp.maximum(place(k) * (Q // 8) - 1, 0)

    return [
        pl.BlockSpec((Q, width), lambda k: (place(k), 1)),
        pl.BlockSpec((8, width), lambda k: (halo(k), 1)),
        pl.BlockSpec((Q, width), lambda k: (place(k), 0)),
        pl.BlockSpec((Q, shared_width), lambda k: (place(k), 0)),
        pl.BlockSpec((8, shared_width), lambda k: (halo(k), 0)),
        pl.BlockSpec((Q, LANES), lambda k: (place(k), 0)),
        pl.BlockSpec((Q, LANES), lambda k: (place(k), 0)),
        pl.BlockSpec((row_heads, Q), lambda k: (0, place(k))),
        pl.BlockSpec((Q, LANES), lambda k: (place(k), 0)),
        pl.BlockSpec((8, Q), lambda k: (0, place(k))),
        pl.BlockSpec((8, width), lambda k: (0, 0)),
        pl.BlockSpec((8, shared_width), lambda k: (0, 0)),
        pl.BlockSpec((LANES, width), lambda k: (0, 0)),
    ]


def mixer_forward(heads, width, args):
    proj, shared = args[0], args[3]
    count, shared_width, row_heads = proj.shape[0], shared.shape[1], args[7].shape[0]
    blocks = count // Q
    return pl.pallas_call(
        functools.partial(forward_kernel, heads),
        grid=(blocks,),
        in_specs=block_specs(width, shared_width, row_heads, blocks, lambda k: k),
        out_specs=[
            pl.BlockSpec((Q, width), lambda k: (k, 0)),
            pl.BlockSpec((LANES, width), lambda k: (k, 0)),
            pl.BlockSpec((Q, LANES), lambda k: (k, 0)),
        ],
        out_shape=[
            jax.ShapeDtypeStruct((count, width), F32),
            jax.ShapeDtypeStruct((blocks * LANES, width), BF16),
            jax.ShapeDtypeStruct((count, LANES), F32),
        ],
        scratch_shapes=[pltpu.VMEM((LANES, width), F32)],
        compiler_params=pltpu.CompilerParams(vmem_limit_bytes=VMEM_LIMIT),
        cost_estimate=pl.CostEstimate(flops=count * width * 1500, bytes_accessed=count * width * 14, transcendentals=count * width * 4),
    )(*args)


def mixer_backward(heads, width, args):
    proj, shared = args[0], args[3]
    count, shared_width, row_heads = proj.shape[0], shared.shape[1], args[7].shape[0]
    blocks = count // Q
    here = lambda k: blocks - 1 - k
    rows = lambda k: (here(k), 0)
    return pl.pallas_call(
        functools.partial(backward_kernel, heads),
        grid=(blocks,),
        in_specs=block_specs(width, shared_width, row_heads, blocks, here)
        + [
            pl.BlockSpec((LANES, width), rows),
            pl.BlockSpec((Q, width), rows),
            pl.BlockSpec((Q, width), rows),
            pl.BlockSpec((Q, LANES), rows),
        ],
        out_specs=[
            pl.BlockSpec((Q, 2 * width), rows),
            pl.BlockSpec((Q, shared_width), rows),
            pl.BlockSpec((Q, LANES), rows),
            pl.BlockSpec((Q, LANES), rows),
            pl.BlockSpec((row_heads, Q), lambda k: (0, here(k))),
            pl.BlockSpec((8, width), lambda k: (0, 0)),
            pl.BlockSpec((8, shared_width), lambda k: (0, 0)),
        ],
        out_shape=[
            jax.ShapeDtypeStruct((count, 2 * width), BF16),
            jax.ShapeDtypeStruct((count, shared_width), F32),
            jax.ShapeDtypeStruct((count, LANES), F32),
            jax.ShapeDtypeStruct((count, LANES), F32),
            jax.ShapeDtypeStruct((row_heads, count), F32),
            jax.ShapeDtypeStruct((8, width), F32),
            jax.ShapeDtypeStruct((8, shared_width), F32),
        ],
        scratch_shapes=[
            pltpu.VMEM((LANES, width), F32),
            pltpu.VMEM((8, width), F32),
            pltpu.VMEM((8, shared_width), F32),
        ],
        compiler_params=pltpu.CompilerParams(vmem_limit_bytes=VMEM_LIMIT),
        cost_estimate=pl.CostEstimate(flops=count * width * 4000, bytes_accessed=count * width * 24, transcendentals=count * width * 5),
    )(*args)


def pad_lanes(value, lanes=LANES):
    return jnp.pad(value, ((0, 0), (0, lanes - value.shape[1])))


def token_columns(seg, heads):
    count = seg.shape[0]
    early = [jnp.concatenate([jnp.full((s,), -1, jnp.int32), seg[:-s]]) == seg for s in (1, 2, 3)]
    late = [jnp.concatenate([seg[s:], jnp.full((s,), -1, jnp.int32)]) == seg for s in (1, 2, 3)]
    by_block = seg.reshape(count // Q, Q)
    prev = jnp.concatenate([jnp.full((1,), -1, jnp.int32), by_block[:-1, -1]])
    enters = (by_block == prev[:, None]).reshape(count)
    leaves = (by_block == by_block[:, -1:]).reshape(count)
    stack = [seg] + early + [enters, leaves] + late
    return pad_lanes(jnp.stack([v.astype(F32) for v in stack], axis=1))


def shards(
    tokens, lengths, cotangent, pre_gain, w_gate, w_inner, w_shared, w_step, conv_inner,
    conv_inner_bias, conv_shared, conv_shared_bias, step_bias, decay_log, skip_gain, mix_gain, w_out,
):
    tensor_count, dp_count = lax.axis_size("tensor"), lax.axis_size("dp")
    everyone = tensor_count * dp_count
    rows_dev, width = tokens.shape
    group = rows_dev * tensor_count
    heads = step_bias.shape[0]
    inner = w_gate.shape[1]
    head_width = inner // heads
    shared_width = w_shared.shape[1]
    inner_all = inner * tensor_count
    row_heads = -(-heads // 8) * 8

    own_w, own_g, own_c = w_shared.shape[0], pre_gain.shape[0], conv_shared.shape[0]
    taps = conv_shared.shape[1]
    extra = jnp.concatenate([pre_gain, conv_shared.reshape(-1), conv_shared_bias])
    extra = jnp.pad(extra, (0, shared_width - extra.shape[0]))[None, :]
    packed_rows = -(-(own_w + 1) // 16) * 16
    packed = jnp.concatenate([w_shared, extra], axis=0)
    packed = jnp.pad(packed, ((0, packed_rows - own_w - 1), (0, 0)))
    packed = lax.all_gather(packed, ("dp", "tensor"), axis=0, tiled=False)
    shared_full = packed[:, :own_w].reshape(width, shared_width)
    extras = packed[:, own_w]
    gain_full = extras[:, :own_g].reshape(-1)
    kernel_shared = extras[:, own_g : own_g + own_c * taps].reshape(shared_width, taps)
    bias_shared = extras[:, own_g + own_c * taps : own_g + own_c * taps + own_c].reshape(-1)

    split_full = lax.all_gather(
        jnp.concatenate([w_gate, w_inner, pad_lanes(w_step)], axis=1), "dp", axis=0, tiled=True
    )
    out_full = lax.all_gather(w_out.T, "dp", axis=0, tiled=True)
    cot_all = lax.all_gather(cotangent, "tensor", axis=0, tiled=True)

    rows = tokens.astype(F32)
    gain_pre = gain_full.astype(F32)[None, :]
    rinv = lax.rsqrt(jnp.mean(rows * rows, axis=-1, keepdims=True) + EPS)
    normed_in = (rows * rinv * gain_pre).astype(BF16)
    gathered = lax.all_gather(normed_in, "tensor", axis=0, tiled=True)
    proj = mul(gathered, split_full[:, : 2 * inner])
    step_raw = mul(gathered, split_full[:, 2 * inner :])[:, :heads]
    shared_pre = mul(gathered, shared_full)
    seg = segment_ids(lengths[0], group)

    shifted_step = step_raw + step_bias[None, :]
    step = jax.nn.softplus(shifted_step)
    decay = -jnp.exp(decay_log)
    rate = step * decay[None, :]
    rate_row = jnp.pad(rate.T, ((0, row_heads - heads), (0, 0)))
    cols = token_columns(seg, heads)
    seg_row = jnp.broadcast_to(seg.astype(F32)[None, :], (8, group))
    channel = jnp.arange(inner)
    low_lanes = (channel % LANES < head_width).astype(F32)
    gain_mix = mix_gain.astype(F32)
    taps_inner = jnp.concatenate(
        [conv_inner.T, jnp.stack([conv_inner_bias, jnp.repeat(skip_gain, head_width), gain_mix, low_lanes])]
    )
    taps_shared = jnp.pad(
        jnp.concatenate([kernel_shared.T, bias_shared[None, :]]).astype(F32), ((0, 7 - taps), (0, 0))
    )
    expand = (jnp.arange(LANES)[:, None] == channel[None, :] // head_width).astype(BF16)
    args = (
        proj, proj, proj, shared_pre, shared_pre, pad_lanes(step), pad_lanes(rate), rate_row,
        cols, seg_row, taps_inner, taps_shared, expand,
    )
    gated, states, sums = mixer_forward(heads, inner, args)

    grad_mixed = mul(cot_all, out_full)
    crosses = jnp.sum(grad_mixed * gain_mix[None, :] * gated, axis=-1)
    square_sum, cross = lax.psum(jnp.stack([sums[:, 0], crosses]), "tensor")
    rmix = lax.rsqrt(square_sum / inner_all + EPS)
    mixed = (gated * rmix[:, None] * gain_mix[None, :]).astype(BF16)
    out_term = contract_first(cot_all, mixed).astype(BF16)
    owned_out = lax.psum_scatter(out_term, "dp", scatter_dimension=0, tiled=True).astype(F32).T
    partial_value = contract_last(mixed, out_full)
    out_rows = lax.psum_scatter(partial_value, "tensor", scatter_dimension=0, tiled=True)
    output = (rows + out_rows).astype(BF16)

    norms = pad_lanes(jnp.stack([rmix, rmix**3 * cross / inner_all], axis=1))
    low, d_shared, d_step_part, d_log, d_log_row, acc_inner, acc_shared = mixer_backward(
        heads, inner, args + (states, grad_mixed, gated, norms)
    )
    d_logs = (d_log[:, :heads] - d_log_row[:heads].T).reshape(group // Q, Q, heads)
    after = (jnp.arange(Q)[:, None] <= jnp.arange(Q)[None, :]).astype(F32)
    d_rate = jnp.einsum("ti,kih->kth", after, d_logs, precision=HIGH).reshape(group, heads)
    d_step = (d_step_part[:, :heads] + d_rate * decay[None, :]) * jax.nn.sigmoid(shifted_step)
    d_decay = jnp.sum(d_rate * step, axis=0) * decay
    step_low = pad_lanes(d_step.astype(BF16))

    back_part = contract_last(low, split_full[:, : 2 * inner]) + contract_last(
        step_low, split_full[:, 2 * inner :]
    )
    split_grad = jnp.concatenate(
        [contract_first(gathered, low).astype(BF16), contract_first(gathered, step_low).astype(BF16)], axis=1
    )
    owned_split = lax.psum_scatter(split_grad, "dp", scatter_dimension=0, tiled=True).astype(F32)
    back_rows = lax.psum_scatter(
        jnp.concatenate([back_part, d_shared], axis=1), "tensor", scatter_dimension=0, tiled=True
    )
    shared_low = back_rows[:, width:].astype(BF16)
    back_rows = back_rows[:, :width] + contract_last(shared_low, shared_full)
    grad_shared_w = contract_first(normed_in, shared_low)
    grad_pre = jnp.sum(back_rows * rows * rinv, axis=0)
    upstream_pre = back_rows * gain_pre
    grad_tokens = (
        upstream_pre * rinv
        - rows * rinv**3 * jnp.sum(upstream_pre * rows, axis=-1, keepdims=True) / width
        + cotangent.astype(F32)
    )
    tail = jnp.concatenate(
        [
            grad_pre.reshape(everyone, own_g),
            acc_shared[:taps].T.reshape(everyone, own_c * taps),
            acc_shared[taps].reshape(everyone, own_c),
        ],
        axis=1,
    )
    tail = pad_lanes(tail, shared_width)[:, None, :]
    back_rows_dev = -(-(own_w + 1) // 8) * 8
    give = jnp.concatenate([grad_shared_w.reshape(everyone, own_w, shared_width), tail], axis=1)
    give = jnp.pad(give, ((0, 0), (0, back_rows_dev - own_w - 1), (0, 0)))
    mine = lax.psum_scatter(
        give.reshape(everyone * back_rows_dev, shared_width), ("dp", "tensor"), scatter_dimension=0, tiled=True
    )
    owned_shared, own_row = mine[:own_w], mine[own_w]
    owned_pre = own_row[:own_g]
    owned_kernel = own_row[own_g : own_g + own_c * taps].reshape(own_c, taps)
    owned_bias = own_row[own_g + own_c * taps : own_g + own_c * taps + own_c]

    heads_row = jnp.concatenate([jnp.sum(d_step, axis=0), d_decay])
    heads_row = jnp.pad(heads_row, (0, inner - 2 * heads))[None, :]
    sums_dp = lax.psum(jnp.concatenate([acc_inner[:7], heads_row], axis=0), "dp")
    return (
        output,
        grad_tokens,
        owned_pre,
        owned_split[:, :inner],
        owned_split[:, inner : 2 * inner],
        owned_shared,
        owned_split[:, 2 * inner : 2 * inner + heads],
        sums_dp[:4].T,
        sums_dp[4],
        owned_kernel,
        owned_bias,
        sums_dp[7, :heads],
        sums_dp[7, heads : 2 * heads],
        sums_dp[5].reshape(heads, head_width).sum(axis=1),
        sums_dp[6],
        owned_out,
    )

def solution(mesh):
    in_specs = (
        P(("dp", "tensor"), None),
        P("dp", None),
        P(("dp", "tensor"), None),
        P(("dp", "tensor")),
        P("dp", "tensor"),
        P("dp", "tensor"),
        P(("dp", "tensor"), None),
        P("dp", "tensor"),
        P("tensor", None),
        P("tensor"),
        P(("dp", "tensor"), None),
        P(("dp", "tensor")),
        P("tensor"),
        P("tensor"),
        P("tensor"),
        P("tensor"),
        P("tensor", "dp"),
    )
    out_specs = (
        P(("dp", "tensor"), None),
        P(("dp", "tensor"), None),
        P(("dp", "tensor")),
        P("dp", "tensor"),
        P("dp", "tensor"),
        P(("dp", "tensor"), None),
        P("dp", "tensor"),
        P("tensor", None),
        P("tensor"),
        P(("dp", "tensor"), None),
        P(("dp", "tensor")),
        P("tensor"),
        P("tensor"),
        P("tensor"),
        P("tensor"),
        P("tensor", "dp"),
    )
    return jax.shard_map(shards, mesh=mesh, in_specs=in_specs, out_specs=out_specs, check_vma=False)
```

time: 1500 us -> 935 us (0.62)
  matrix products: 357 us -> 102 us
  local copies, waits for them, and re-layouts: 281 us -> 33 us
  waiting for transfers between devices: 331 us -> 515 us
  other arithmetic: 200 us -> 30.3 us
  blocking collectives: 302 us -> 142 us
  Pallas kernels: 0 us -> 93 us
    dot_general x34 -> x13, matrix products: 347 us -> 102 us  [the longest x4 36.9 us: mul(): return jnp.dot(left, right, preferred_element_type=F32)]
    reshape x13 -> x6, local copies, waits for them, and re-layouts: 111 us -> 0.52 us  [the longest x2 0.18 us: shards(): extras[:, own_g:own_g + own_c * taps].reshape(shared_width, taps)]
    pallas_call x0 -> x2, Pallas kernels: none -> 93 us  [the longest x1 64.8 us: mixer_backward(): pl.pallas_call(functools.partial(backward_kernel, heads), grid=(blocks,),...]
    unnamed x2 -> x0, blocking collectives: 82.1 us -> none
    all_gather x3 -> x1, blocking collectives: 151 us -> 73.9 us  [shards(): packed = lax.all_gather(packed, ('dp', 'tensor'), axis=0, tiled=False)]
    reduce_sum x16 -> x2, other arithmetic: 69.8 us -> 1.77 us  [the longest x1 1.14 us: shards(): heads_row = jnp.concatenate([jnp.sum(d_step, axis=0), d_decay])]
    dynamic_slice x32 -> x0, local copies, waits for them, and re-layouts: 52.6 us -> none  [blockwise_scan(): lax.scan(carry_step, jnp.zeros((heads, states, width), jnp.float32), (car...]
    all_gather x3 -> x2, waiting for transfers between devices: 0.04 us -> 50 us  [the longest x1 49.9 us: shards(): lax.all_gather(jnp.concatenate([w_gate, w_inner, pad_lanes(w_step)], axis...]
  transfers between devices with their start and end apart: 13 -> 9, of which waited for: 4 -> 7; matrix products, arithmetic and copies ran while one was open for 33% -> 11% of each run, Pallas kernels for 0% -> 3%
where the time goes in v1:
time: 935 us; the launch traced here: 930 us
  waiting for transfers between devices  515 us (55%)
  blocking collectives  142 us (15%)
  matrix products  102 us (11%)
  Pallas kernels  93 us (10%)
  local copies, waits for them, and re-layouts  33 us (4%)
  other arithmetic  30.3 us (3%)
  between operations  14.5 us (2%)
    reduce_scatter x1, waiting for transfers between devices, shards(): lax.psum_scatter(give.reshape(everyone * back_rows_dev, shared_width), ('...  131 us
    reduce_scatter x1, waiting for transfers between devices, shards(): lax.psum_scatter(partial_value, 'tensor', scatter_dimension=0, tiled=True)  97.5 us
    reduce_scatter x1, waiting for transfers between devices, shards(): lax.psum_scatter(jnp.concatenate([back_part, d_shared], axis=1), 'tensor'...  76.9 us
    all_gather x1, blocking collectives, shards(): packed = lax.all_gather(packed, ('dp', 'tensor'), axis=0, tiled=False)  73.9 us
    reduce_scatter x1, waiting for transfers between devices, shards(): lax.psum_scatter(split_grad, 'dp', scatter_dimension=0, tiled=True)  66.7 us
    pallas_call x1, Pallas kernels, mixer_backward(): pl.pallas_call(functools.partial(backward_kernel, heads), grid=(blocks,),...  64.8 us
    psum x1, blocking collectives, shards(): lax.psum(jnp.concatenate([acc_inner[:7], heads_row], axis=0), 'dp')  61.5 us
    all_gather x1, waiting for transfers between devices, shards(): lax.all_gather(jnp.concatenate([w_gate, w_inner, pad_lanes(w_step)], axis...  49.9 us
  transfers between devices with their start and end apart: 9, of which 7 were waited for; matrix products, arithmetic and copies ran while one was open for 11% of the time, Pallas kernels for 3%

profile of v1, /device:TPU:0, one launch (start us, length us, event | category | flops | bytes accessed | tf_op | source)
XLA Modules:
  0.0 930.4 jit_solution(12072016814179453273)
XLA Ops:
  12.4 73.9 %all-gather = bf16[1536,256]{1,0:T(8,128)(2,1)S(1)} all-gather(bf16[48,256]{1,0:T(8,128)(2,1)S(1)} %fusion.34), channel_id=2, replica_groups=mesh['dp'=16,'tensor'=2] {'dp','tensor'}, dimensions={0}, use_global_device_ids=true | all-gather | bytes 811008 | tf_op jit(solution)/shard_map/all_gather | solution.py:381
  97.1 44.1 %all-gather.6.cloned.1.call-done = bf16[2048,1024]{1,0:T(8,128)(2,1)} async-done(((bf16[1024,1024]{1,0:T(8,128)(2,1)}), bf16[2048,1024]{1,0:T(8,128)(2,1)}) %all-gather.6.cloned.1.call-update) | async-done | bytes 4194320 | tf_op jit(solution)/shard_map/all_gather | solution.py:398
  141.2 4.9 fusion.68.sh_ref.halo_sh_ref
  146.1 49.9 %all-gather.8.cloned.1.call-done = bf16[1024,2176]{1,0:T(8,128)(2,1)} async-done(((bf16[64,2176]{1,0:T(8,128)(2,1)}), bf16[1024,2176]{1,0:T(8,128)(2,1)}) %all-gather.8.cloned.1.call-update) | async-done | bytes 4456464 | tf_op jit(solution)/shard_map/all_gather | solution.py:388
  202.3 15.4 %fusion.13.pre_ref.halo_ref.gate_ref = f32[2048,2048]{1,0:T(8,128)} fusion(bf16[2048,1024]{1,0:T(8,128)(2,1)} %all-gather.6.cloned.1.call-done, bf16[1024,2176]{1,0:T(8,128)(2,1)} %all-gather.8.cloned.1.call-done), kind=kOutput, calls=%fused_computation.26 | convolution fusion | flops 8589934592 | bytes 25165824 | tf_op jit(solution)/shard_map/dot_general | solution.py:36
  218.3 28.2 %shard_map.288 = (f32[2048,1024]{1,0:T(8,128)}, bf16[2048,1024]{1,0:T(8,128)(2,1)}, f32[2048,128]{1,0:T(8,128)}) custom-call(f32[2048,2048]{1,0:T(8,128)} %fusion.13.pre_ref.halo_ref.gate_ref, f32[2048,2048]{1,0:T(8,128)} %fusion.13.pre_ref.halo_ref.gate_ref, f32[2048,2048]{1,0:T(8,128)} %fusion.13.pre_ref.halo_ref.gate_ref, ...), custom_call_target="tpu_custom_call" | custom-call | flops 3145728000 | bytes 29360128 | tf_op jit(solution)/shard_map/pallas_call | solution.py:279
  248.2 46.9 %all-gather.10.cloned.1.call-done = bf16[2048,1024]{1,0:T(8,128)(2,1)} async-done(((bf16[1024,1024]{1,0:T(8,128)(2,1)}), bf16[2048,1024]{1,0:T(8,128)(2,1)}) %all-gather.10.cloned.1.call-update) | async-done | bytes 4194320 | tf_op jit(solution)/shard_map/all_gather | solution.py:392
  295.2 13.2 %multiply_reduce_fusion = (f32[2048]{0:T(1024)S(1)}, f32[2048,1024]{1,0:T(8,128)}) fusion(f32[2048,1024]{1,0:T(8,128)} %get-tuple-element.26.gated_ref, f32[1024]{0:T(1024)S(1)} %copy-done.9, bf16[2048,1024]{1,0:T(8,128)(2,1)} %all-gather.10.cloned.1.call-done, bf16[1024,1024]{1,0:T(8,128)(2,1)} %all-gather.12.cloned.1.call-done), kind=kOutput, calls=%fused_computation.8 | convolution fusion | flops 4301256704 | bytes 23080960 | tf_op jit(solution)/shard_map/dot_general | solution.py:36
  308.4 7.0 psum.14
  316.8 64.8 %shard_map.289 = (bf16[2048,2048]{1,0:T(8,128)(2,1)}, f32[2048,256]{1,0:T(8,128)}, f32[2048,128]{1,0:T(8,128)}, f32[2048,128]{1,0:T(8,128)}, f32[16,2048]{1,0:T(...) custom-call(f32[2048,2048]{1,0:T(8,128)} %fusion.13.pre_ref.halo_ref.gate_ref, ...), custom_call_target="tpu_custom_call" | custom-call | flops 8388608000 | bytes 50331648 | tf_op jit(solution)/shard_map/pallas_call | solution.py:305
  387.2 12.6 %fusion.11 = f32[2048,1024]{1,0:T(8,128)S(1)} fusion(bf16[2048,2048]{1,0:T(8,128)(2,1)} %get-tuple-element.29, bf16[1024,2176]{1,0:T(8,128)(2,1)} %all-gather.8.cloned.1.call-done), kind=kOutput, calls=%fused_computation.24 | convolution fusion | flops 8589934592 | bytes 20971520 | tf_op jit(solution)/shard_map/dot_general | solution.py:28
  399.7 5.5 convolution_add_fusion
  405.2 9.1 pad_maximum_fusion
  414.8 10.8 %convert_bitcast_fusion = bf16[1024,1024]{0,1:T(8,128)(2,1)} fusion(bf16[2048,1024]{1,0:T(8,128)(2,1)} %all-gather.10.cloned.1.call-done, f32[2048,1024]{1,0:T(8,128)} %get-tuple-element.26.gated_ref, f32[2048]{0:T(1024)S(1)} %bitcast.126, f32[1024]{0:T(1024)S(1)} %copy-done.9), kind=kOutput, calls=%fused_computation.29 | convolution fusion | flops 4302307328 | bytes 14692352 | tf_op jit(solution)/shard_map/dot_general | solution.py:32
  425.6 3.9 copy.184
  433.3 11.7 %convolution_convert_fusion = bf16[1024,2048]{1,0:T(8,128)(2,1)S(1)} fusion(bf16[2048,1024]{1,0:T(8,128)(2,1)S(1)} %copy-done.1, bf16[2048,2048]{1,0:T(8,128)(2,1)} %get-tuple-element.29), kind=kOutput, calls=%fused_computation.23 | convolution fusion | flops 8592031744 | bytes 16777216 | tf_op jit(solution)/shard_map/dot_general | solution.py:32
  447.9 11.8 %fusion.58 = f32[2048,1024]{1,0:T(8,128)} fusion(bf16[1024,1024]{1,0:T(8,128)(2,1)} %all-gather.12.cloned.1.call-done, f32[2048,1024]{1,0:T(8,128)} %get-tuple-element.26.gated_ref, f32[2048]{0:T(1024)S(1)} %bitcast.127, f32[1024]{0:T(1024)S(1)} %copy-done.9), kind=kOutput, calls=%fused_computation.134 | convolution fusion | flops 4301258752 | bytes 18886656 | tf_op jit(solution)/shard_map/dot_general | solution.py:28
  460.7 76.9 %reduce-scatter.10.cloned.1.call-done = f32[1024,1280]{1,0:T(8,128)} async-done(((f32[2048,1280]{1,0:T(8,128)}), f32[1024,1280]{1,0:T(8,128)}) %reduce-scatter.10.cloned.1.call-update) | async-done | bytes 5242896 | tf_op jit(solution)/shard_map/reduce_scatter | solution.py:456
  537.6 5.9 fusion.10
  547.7 61.5 %psum.15 = f32[8,1024]{1,0:T(8,128)S(1)} all-reduce(f32[8,1024]{1,0:T(8,128)S(1)} %pad_maximum_fusion.2), channel_id=1, replica_groups=mesh['dp'=16,'tensor'=2] {'dp'}, use_global_device_ids=true, to_apply=%region_13.14 | all-reduce | flops 8192 | bytes 65536 | tf_op jit(solution)/shard_map/psum | solution.py:491
  613.7 66.7 %reduce-scatter.14.cloned.1.call-done = bf16[64,2176]{1,0:T(8,128)(2,1)} async-done(((bf16[1024,2176]{1,0:T(8,128)(2,1)}), bf16[64,2176]{1,0:T(8,128)(2,1)}) %reduce-scatter.14.cloned.1.call-update) | async-done | bytes 278544 | tf_op jit(solution)/shard_map/reduce_scatter | solution.py:455
  683.6 97.5 %reduce-scatter.8.cloned.1.call-done = f32[1024,1024]{1,0:T(8,128)} async-done(((f32[2048,1024]{1,0:T(8,128)}), f32[1024,1024]{1,0:T(8,128)}) %reduce-scatter.8.cloned.1.call-update) | async-done | bytes 4194320 | tf_op jit(solution)/shard_map/reduce_scatter | solution.py:435
  781.1 6.5 fusion.7
  787.7 131.3 %reduce-scatter.12.cloned.1.call-done = f32[40,256]{1,0:T(8,128)} async-done(((f32[1280,256]{1,0:T(8,128)}), f32[40,256]{1,0:T(8,128)}) %reduce-scatter.12.cloned.1.call-update) | async-done | bytes 40976 | tf_op jit(solution)/shard_map/reduce_scatter | solution.py:481
  (158 shorter events, 55.8 us)
Async XLA Ops:
  7.2 79.4 %copy-start = (bf16[1024,1024]{1,0:T(8,128)(2,1)S(1)}, bf16[1024,1024]{1,0:T(8,128)(2,1)}, u32[]{:S(2)}) copy-start(bf16[1024,1024]{1,0:T(8,128)(2,1)} %param.17) | copy-start | bytes 6291460
  7.2 134.0 %all-gather.6.cloned.1.call-start = ((), (), s32[]{:S(2)}) async-start(), calls=%async_computation.5 | async-start | bytes 6291456 | tf_op jit(solution)/shard_map/all_gather | solution.py:398
  11.1 77.5 %copy-start.12 = (bf16[64,16]{0,1:T(8,128)(2,1)S(1)}, bf16[64,16]{0,1:T(8,128)(2,1)}, u32[]{:S(2)}) copy-start(bf16[64,16]{0,1:T(8,128)(2,1)} %param.24) | copy-start | bytes 6148
  11.1 77.6 %copy-start.4 = (bf16[64,1024]{1,0:T(8,128)(2,1)S(1)}, bf16[64,1024]{1,0:T(8,128)(2,1)}, u32[]{:S(2)}) copy-start(bf16[64,1024]{1,0:T(8,128)(2,1)} %param.22) | copy-start | bytes 393220
  11.1 77.5 %copy-start.5 = (bf16[64,1024]{1,0:T(8,128)(2,1)S(1)}, bf16[64,1024]{1,0:T(8,128)(2,1)}, u32[]{:S(2)}) copy-start(bf16[64,1024]{1,0:T(8,128)(2,1)} %param.21) | copy-start | bytes 393220
  88.4 6.6 copy-start.10
  88.4 6.6 copy-start.13
  88.5 7.9 copy-start.21
  88.5 107.6 %all-gather.8.cloned.1.call-start = ((), (), s32[]{:S(2)}) async-start(), calls=%async_computation.6 | async-start | bytes 4734976 | tf_op jit(solution)/shard_map/all_gather | solution.py:388
  89.4 158.8 %all-gather.12.cloned.1.call-start = ((), (), s32[]{:S(2)}) async-start(), calls=%async_computation.8 | async-start | bytes 2228224 | tf_op jit(solution)/shard_map/all_gather | solution.py:391
  90.1 205.0 %all-gather.10.cloned.1.call-start = ((), (), s32[]{:S(2)}) async-start(), calls=%async_computation.7 | async-start | bytes 6291456 | tf_op jit(solution)/shard_map/all_gather | solution.py:392
  90.7 446.9 %reduce-scatter.10.cloned.1.call-start = ((), (), s32[]{:S(2)}) async-start(), calls=%async_computation.10 | async-start | bytes 15728640 | tf_op jit(solution)/shard_map/reduce_scatter | solution.py:456
  92.6 53.5 %copy-start.8 = (f32[1024]{0:T(1024)}, f32[1024]{0:T(1024)S(1)}, u32[]{:S(2)}) copy-start(f32[1024]{0:T(1024)S(1)} %convert_element_type.163) | copy-start | bytes 12292
  95.0 101.0 %copy-start.19 = (f32[16]{0:T(128)S(1)}, f32[16]{0:T(128)}, u32[]{:S(2)}) copy-start(f32[16]{0:T(128)} %param.29) | copy-start | bytes 196
  96.3 103.2 %copy-start.16 = (f32[16]{0:T(128)}, f32[16]{0:T(128)S(1)}, u32[]{:S(2)}) copy-start(f32[16]{0:T(128)S(1)} %exponential_negate_fusion) | copy-start | bytes 196
  199.5 18.1 %copy-start.2 = (f32[2048,16]{0,1:T(8,128)}, f32[2048,16]{0,1:T(8,128)S(1)}, u32[]{:S(2)}) copy-start(f32[2048,16]{0,1:T(8,128)S(1)} %get-tuple-element.127) | copy-start | bytes 393220
  218.3 76.9 %copy-start.9 = (f32[1024]{0:T(1024)S(1)}, f32[1024]{0:T(1024)}, u32[]{:S(2)}) copy-start(f32[1024]{0:T(1024)} %copy-done.8) | copy-start | bytes 12292
  381.6 4.4 copy-start.17
  414.4 197.3 %reduce-scatter.16.cloned.1.call-start = ((), (), s32[]{:S(2)}) async-start(), calls=%async_computation.13 | async-start | bytes 2228224
  429.6 250.9 %reduce-scatter.14.cloned.1.call-start = ((), (), s32[]{:S(2)}) async-start(), calls=%async_computation.12 | async-start | bytes 4734976 | tf_op jit(solution)/shard_map/reduce_scatter | solution.py:455
  447.7 333.4 %reduce-scatter.8.cloned.1.call-start = ((), (), s32[]{:S(2)}) async-start(), calls=%async_computation.9 | async-start | bytes 12582912 | tf_op jit(solution)/shard_map/reduce_scatter | solution.py:435
  459.7 77.9 %copy-start.3 = (bf16[32,32,256]{2,1,0:T(8,128)(2,1)S(1)}, bf16[32,32,256]{2,1,0:T(8,128)(2,1)}, u32[]{:S(2)}) copy-start(bf16[32,32,256]{2,1,0:T(8,128)(2,1)} %slice.169) | copy-start | bytes 1572868
  459.7 459.3 %reduce-scatter.12.cloned.1.call-start = ((), (), s32[]{:S(2)}) async-start(), calls=%async_computation.11 | async-start | bytes 1351680 | tf_op jit(solution)/shard_map/reduce_scatter | solution.py:481
  546.4 234.8 %copy-start.11 = (f32[1024]{0:T(1024)S(1)}, f32[1024]{0:T(1024)}, u32[]{:S(2)}) copy-start(f32[1024]{0:T(1024)} %get-tuple-element.152) | copy-start | bytes 12292
  (8 other events, 29.0 us)
Sparse Core Ops, SparseCore 0:
  88.6 52.6 all-gather.5
  144.1 51.9 all-gather.7
  198.2 39.9 all-gather.11
  239.6 55.5 all-gather.9
  414.5 123.0 reduce-scatter.9
  541.2 61.8 reduce-scatter.15
  607.4 72.9 reduce-scatter.13
  682.7 98.3 reduce-scatter.7
  783.5 135.4 reduce-scatter.11

commit v2 on v1

--- a/solution.py
+++ b/solution.py
@@ -378,7 +378,8 @@
     packed_rows = -(-(own_w + 1) // 16) * 16
     packed = jnp.concatenate([w_shared, extra], axis=0)
     packed = jnp.pad(packed, ((0, packed_rows - own_w - 1), (0, 0)))
-    packed = lax.all_gather(packed, ("dp", "tensor"), axis=0, tiled=False)
+    packed = lax.all_gather(lax.all_gather(packed, "tensor", axis=0, tiled=True), "dp", axis=0, tiled=True)
+    packed = packed.reshape(everyone, packed_rows, shared_width)
     shared_full = packed[:, :own_w].reshape(width, shared_width)
     extras = packed[:, own_w]
     gain_full = extras[:, :own_g].reshape(-1)
@@ -395,7 +396,9 @@
     gain_pre = gain_full.astype(F32)[None, :]
     rinv = lax.rsqrt(jnp.mean(rows * rows, axis=-1, keepdims=True) + EPS)
     normed_in = (rows * rinv * gain_pre).astype(BF16)
-    gathered = lax.all_gather(normed_in, "tensor", axis=0, tiled=True)
+    rows_all = lax.all_gather(tokens, "tensor", axis=0, tiled=True).astype(F32)
+    rinv_all = lax.rsqrt(jnp.mean(rows_all * rows_all, axis=-1, keepdims=True) + EPS)
+    gathered = (rows_all * rinv_all * gain_pre).astype(BF16)
     proj = mul(gathered, split_full[:, : 2 * inner])
     step_raw = mul(gathered, split_full[:, 2 * inner :])[:, :heads]
     shared_pre = mul(gathered, shared_full)
@@ -430,9 +433,10 @@
     rmix = lax.rsqrt(square_sum / inner_all + EPS)
     mixed = (gated * rmix[:, None] * gain_mix[None, :]).astype(BF16)
     out_term = contract_first(cot_all, mixed).astype(BF16)
+    partial_value = contract_last(mixed, out_full)
+    rmix, cross, partial_value, out_term = lax.optimization_barrier((rmix, cross, partial_value, out_term))
+    out_rows = lax.psum_scatter(partial_value, "tensor", scatter_dimension=0, tiled=True)
     owned_out = lax.psum_scatter(out_term, "dp", scatter_dimension=0, tiled=True).astype(F32).T
-    partial_value = contract_last(mixed, out_full)
-    out_rows = lax.psum_scatter(partial_value, "tensor", scatter_dimension=0, tiled=True)
     output = (rows + out_rows).astype(BF16)
 
     norms = pad_lanes(jnp.stack([rmix, rmix**3 * cross / inner_all], axis=1))
@@ -479,8 +483,9 @@
     give = jnp.concatenate([grad_shared_w.reshape(everyone, own_w, shared_width), tail], axis=1)
     give = jnp.pad(give, ((0, 0), (0, back_rows_dev - own_w - 1), (0, 0)))
     mine = lax.psum_scatter(
-        give.reshape(everyone * back_rows_dev, shared_width), ("dp", "tensor"), scatter_dimension=0, tiled=True
-    )
+        give.reshape(everyone * back_rows_dev, shared_width), "dp", scatter_dimension=0, tiled=True
+    )
+    mine = lax.psum_scatter(mine, "tensor", scatter_dimension=0, tiled=True)
     owned_shared, own_row = mine[:own_w], mine[own_w]
     owned_pre = own_row[:own_g]
     owned_kernel = own_row[own_g : own_g + own_c * taps].reshape(own_c, taps)
@@ -488,7 +493,8 @@
 
     heads_row = jnp.concatenate([jnp.sum(d_step, axis=0), d_decay])
     heads_row = jnp.pad(heads_row, (0, inner - 2 * heads))[None, :]
-    sums_dp = lax.psum(jnp.concatenate([acc_inner[:7], heads_row], axis=0), "dp")
+    own_sums = jnp.concatenate([acc_inner[:7], heads_row], axis=0)
+    sums_dp = jnp.sum(lax.all_gather(own_sums, "dp", axis=0, tiled=True).reshape(dp_count, 8, inner), axis=0)
     return (
         output,
         grad_tokens,

time: 935 us -> 819 us (0.88)
  blocking collectives: 142 us -> 59.6 us
  waiting for transfers between devices: 515 us -> 484 us
    reduce_scatter x1 -> x2, waiting for transfers between devices: 131 us -> 63.3 us  [the longest x1 57.8 us: shards(): lax.psum_scatter(give.reshape(everyone * back_rows_dev, shared_width), 'd...]
    psum x1 -> x0, blocking collectives: 61.5 us -> none  [shards(): lax.psum(jnp.concatenate([acc_inner[:7], heads_row], axis=0), 'dp')]
    unnamed x10 -> x11, waiting for transfers between devices: 1.32 us -> 32.7 us
    all_gather x1, waiting for transfers between devices: 44.1 us -> 21.3 us  [shards(): rows_all = lax.all_gather(tokens, 'tensor', axis=0, tiled=True).astype(F32)]
    reduce_scatter x1, waiting for transfers between devices: 76.9 us -> 98.4 us  [shards(): lax.psum_scatter(jnp.concatenate([back_part, d_shared], axis=1), 'tensor'...]
    all_gather x1 -> x3, blocking collectives: 73.9 us -> 52.7 us  [the longest x1 24.4 us: shards(): lax.all_gather(lax.all_gather(packed, 'tensor', axis=0, tiled=True), 'dp'...]
  transfers between devices with their start and end apart: 9 -> 10, of which waited for: 7 -> 9; matrix products, arithmetic and copies ran while one was open for 11% -> 10% of each run, Pallas kernels for 3% -> 4%
where the time goes in v2:
time: 819 us; the launch traced here: 810 us
  waiting for transfers between devices  484 us (59%)
  matrix products  94.9 us (12%)
  Pallas kernels  93 us (11%)
  blocking collectives  59.6 us (7%)
  local copies, waits for them, and re-layouts  34.2 us (4%)
  other arithmetic  28.5 us (3%)
  between operations  15 us (2%)
    reduce_scatter x1, waiting for transfers between devices, shards(): lax.psum_scatter(partial_value, 'tensor', scatter_dimension=0, tiled=True)  101 us
    reduce_scatter x1, waiting for transfers between devices, shards(): lax.psum_scatter(jnp.concatenate([back_part, d_shared], axis=1), 'tensor'...  98.4 us
    reduce_scatter x1, waiting for transfers between devices, shards(): lax.psum_scatter(split_grad, 'dp', scatter_dimension=0, tiled=True)  75.5 us
    pallas_call x1, Pallas kernels, mixer_backward(): pl.pallas_call(functools.partial(backward_kernel, heads), grid=(blocks,),...  64.6 us
    reduce_scatter x1, waiting for transfers between devices, shards(): lax.psum_scatter(give.reshape(everyone * back_rows_dev, shared_width), 'd...  57.8 us
    all_gather x1, waiting for transfers between devices, shards(): cot_all = lax.all_gather(cotangent, 'tensor', axis=0, tiled=True)  46.8 us
    all_gather x1, waiting for transfers between devices, shards(): lax.all_gather(jnp.concatenate([w_gate, w_inner, pad_lanes(w_step)], axis...  45.1 us
    dot_general x4, matrix products, mul(): return jnp.dot(left, right, preferred_element_type=F32)  34.4 us
  transfers between devices with their start and end apart: 10, of which 9 were waited for; matrix products, arithmetic and copies ran while one was open for 10% of the time, Pallas kernels for 4%

profile of v2, /device:TPU:0, one launch (start us, length us, event | category | flops | bytes accessed | tf_op | source)
XLA Modules:
  0.0 809.8 jit_solution(4679123093971756541)
XLA Ops:
  18.6 24.4 %all_gather.23 = bf16[1536,256]{1,0:T(8,128)(2,1)S(1)} all-gather(bf16[96,256]{1,0:T(8,128)(2,1)S(1)} %all_gather.22), channel_id=1, replica_groups=mesh['dp'=16,'tensor'=2] {'dp'}, dimensions={0}, use_global_device_ids=true | all-gather | bytes 835584 | tf_op jit(solution)/shard_map/all_gather | solution.py:381
  47.8 21.3 %all-gather.5.cloned.1.call-done = bf16[2048,1024]{1,0:T(8,128)(2,1)} async-done(((bf16[1024,1024]{1,0:T(8,128)(2,1)}), bf16[2048,1024]{1,0:T(8,128)(2,1)}) %all-gather.5.cloned.1.call-update) | async-done | bytes 4194320 | tf_op jit(solution)/shard_map/all_gather | solution.py:399
  78.3 45.1 %all-gather.7.cloned.1.call-done = bf16[1024,2176]{1,0:T(8,128)(2,1)} async-done(((bf16[64,2176]{1,0:T(8,128)(2,1)}), bf16[1024,2176]{1,0:T(8,128)(2,1)}) %all-gather.7.cloned.1.call-update) | async-done | bytes 4456464 | tf_op jit(solution)/shard_map/all_gather | solution.py:389
  129.7 15.2 %fusion.16.pre_ref.halo_ref.gate_ref = f32[2048,2048]{1,0:T(8,128)} fusion(bf16[2048,1024]{1,0:T(8,128)(2,1)} %copy-done.2, bf16[1024,2176]{1,0:T(8,128)(2,1)} %all-gather.7.cloned.1.call-done), kind=kOutput, calls=%fused_computation.31 | convolution fusion | flops 8589934592 | bytes 25165824 | tf_op jit(solution)/shard_map/dot_general | solution.py:36
  145.5 28.4 %shard_map.288 = (f32[2048,1024]{1,0:T(8,128)}, bf16[2048,1024]{1,0:T(8,128)(2,1)}, f32[2048,128]{1,0:T(8,128)}) custom-call(f32[2048,2048]{1,0:T(8,128)} %fusion.16.pre_ref.halo_ref.gate_ref, f32[2048,2048]{1,0:T(8,128)} %fusion.16.pre_ref.halo_ref.gate_ref, f32[2048,2048]{1,0:T(8,128)} %fusion.16.pre_ref.halo_ref.gate_ref, ...), custom_call_target="tpu_custom_call" | custom-call | flops 3145728000 | bytes 29360128 | tf_op jit(solution)/shard_map/pallas_call | solution.py:279
  175.7 46.8 %all-gather.9.cloned.1.call-done = bf16[2048,1024]{1,0:T(8,128)(2,1)} async-done(((bf16[1024,1024]{1,0:T(8,128)(2,1)}), bf16[2048,1024]{1,0:T(8,128)(2,1)}) %all-gather.9.cloned.1.call-update) | async-done | bytes 4194320 | tf_op jit(solution)/shard_map/all_gather | solution.py:393
  222.5 13.2 %multiply_reduce_fusion = (f32[2048]{0:T(1024)S(1)}, f32[2048,1024]{1,0:T(8,128)}) fusion(f32[2048,1024]{1,0:T(8,128)} %get-tuple-element.31.gated_ref, f32[1024]{0:T(1024)S(1)} %convert_element_type.170, bf16[2048,1024]{1,0:T(8,128)(2,1)} %all-gather.9.cloned.1.call-done, bf16[1024,1024]{1,0:T(8,128)(2,1)} %all-gather.11.cloned.1.call-done), kind=kOutput, calls=%fused_computation.13 | convolution fusion | flops 4301256704 | bytes 23080960 | tf_op jit(solution)/shard_map/dot_general | solution.py:36
  235.7 7.0 psum.7
  242.7 11.0 %convert_bitcast_fusion = bf16[1024,1024]{0,1:T(8,128)(2,1)} fusion(bf16[2048,1024]{1,0:T(8,128)(2,1)} %all-gather.9.cloned.1.call-done, f32[2048,1024]{1,0:T(8,128)} %get-tuple-element.31.gated_ref, f32[2048]{0:T(1024)S(1)} %bitcast.111, f32[1024]{0:T(1024)S(1)} %convert_element_type.170), kind=kOutput, calls=%fused_computation.37 | convolution fusion | flops 4302307328 | bytes 14692352 | tf_op jit(solution)/shard_map/dot_general | solution.py:32
  253.7 7.5 fusion.64
  262.6 64.6 %shard_map.289 = (bf16[2048,2048]{1,0:T(8,128)(2,1)}, f32[2048,256]{1,0:T(8,128)}, f32[2048,128]{1,0:T(8,128)}, f32[2048,128]{1,0:T(8,128)}, f32[16,2048]{1,0:T(...) custom-call(f32[2048,2048]{1,0:T(8,128)} %fusion.16.pre_ref.halo_ref.gate_ref, ...), custom_call_target="tpu_custom_call" | custom-call | flops 8388608000 | bytes 50331648 | tf_op jit(solution)/shard_map/pallas_call | solution.py:305
  330.9 12.7 %fusion.14 = f32[2048,1024]{1,0:T(8,128)S(1)} fusion(bf16[2048,2048]{1,0:T(8,128)(2,1)} %get-tuple-element.36, bf16[1024,2176]{1,0:T(8,128)(2,1)} %all-gather.7.cloned.1.call-done), kind=kOutput, calls=%fused_computation.29 | convolution fusion | flops 8589934592 | bytes 20971520 | tf_op jit(solution)/shard_map/dot_general | solution.py:28
  343.6 5.6 convolution_add_fusion
  349.2 8.5 %pad_maximum_fusion = f32[2048,1280]{1,0:T(8,128)} fusion(f32[2048,256]{1,0:T(8,128)S(1)} %copy-done.6, f32[2048,1024]{1,0:T(8,128)} %convolution_add_fusion), kind=kLoop, calls=%fused_computation.2 | loop fusion | flops 2621440 | bytes 20971520 | tf_op jit(solution)/shard_map/concatenate | solution.py:461
  365.8 11.8 %convolution_convert_fusion = bf16[1024,2048]{1,0:T(8,128)(2,1)S(1)} fusion(bf16[2048,1024]{1,0:T(8,128)(2,1)S(1)} %copy-done.3, bf16[2048,2048]{1,0:T(8,128)(2,1)} %get-tuple-element.36), kind=kOutput, calls=%fused_computation.28 | convolution fusion | flops 8592031744 | bytes 16777216 | tf_op jit(solution)/shard_map/dot_general | solution.py:32
  382.5 98.4 %reduce-scatter.11.cloned.1.call-done = f32[1024,1280]{1,0:T(8,128)} async-done(((f32[2048,1280]{1,0:T(8,128)}), f32[1024,1280]{1,0:T(8,128)}) %reduce-scatter.11.cloned.1.call-update) | async-done | bytes 5242896 | tf_op jit(solution)/shard_map/reduce_scatter | solution.py:460
  480.9 5.9 fusion.13
  491.4 22.8 %all_gather.27 = f32[128,1024]{1,0:T(8,128)S(1)} all-gather(f32[8,1024]{1,0:T(8,128)S(1)} %pad_maximum_fusion.2), channel_id=1, replica_groups=mesh['dp'=16,'tensor'=2] {'dp'}, dimensions={0}, use_global_device_ids=true | all-gather | bytes 557056 | tf_op jit(solution)/shard_map/all_gather | solution.py:497
  516.8 30.0 %reduce-scatter.19.cloned.1.call-done = bf16[64,1024]{1,0:T(8,128)(2,1)} async-done(((bf16[1024,1024]{1,0:T(8,128)(2,1)}), bf16[64,1024]{1,0:T(8,128)(2,1)}) %reduce-scatter.19.cloned.1.call-update) | async-done | bytes 131088
  548.8 75.5 %reduce-scatter.17.cloned.1.call-done = bf16[64,2176]{1,0:T(8,128)(2,1)} async-done(((bf16[1024,2176]{1,0:T(8,128)(2,1)}), bf16[64,2176]{1,0:T(8,128)(2,1)}) %reduce-scatter.17.cloned.1.call-update) | async-done | bytes 278544 | tf_op jit(solution)/shard_map/reduce_scatter | solution.py:459
  627.5 57.8 %reduce-scatter.13.cloned.1.call-done = f32[80,256]{1,0:T(8,128)} async-done(((f32[1280,256]{1,0:T(8,128)}), f32[80,256]{1,0:T(8,128)}) %reduce-scatter.13.cloned.1.call-update) | async-done | bytes 81936 | tf_op jit(solution)/shard_map/reduce_scatter | solution.py:485
  685.3 100.8 %reduce-scatter.9.cloned.1.call-done = f32[1024,1024]{1,0:T(8,128)} async-done(((f32[2048,1024]{1,0:T(8,128)}), f32[1024,1024]{1,0:T(8,128)}) %reduce-scatter.9.cloned.1.call-update) | async-done | bytes 4194320 | tf_op jit(solution)/shard_map/reduce_scatter | solution.py:438
  786.1 6.5 fusion.8
  792.6 5.5 reduce-scatter.15.cloned.1.call-done
  (168 shorter events, 68.5 us)
Async XLA Ops:
  7.2 5.6 copy-start.15
  7.2 5.8 copy-start.17
  7.2 5.8 copy-start.18
  7.2 5.9 copy-start.10
  7.2 36.0 %copy-start.22 = (f32[16]{0:T(128)S(1)}, f32[16]{0:T(128)}, u32[]{:S(2)}) copy-start(f32[16]{0:T(128)} %param.30) | copy-start | bytes 196
  7.2 36.0 %copy-start.14 = (bf16[1024]{0:T(1024)(128)(2,1)S(1)}, bf16[1024]{0:T(1024)(128)(2,1)}, u32[]{:S(2)}) copy-start(bf16[1024]{0:T(1024)(128)(2,1)} %param.32) | copy-start | bytes 6148
  7.3 36.0 %copy-start.16 = (f32[16]{0:T(128)S(1)}, f32[16]{0:T(128)}, u32[]{:S(2)}) copy-start(f32[16]{0:T(128)} %param.31) | copy-start | bytes 196
  7.3 61.9 %all-gather.5.cloned.1.call-start = ((), (), s32[]{:S(2)}) async-start(), calls=%async_computation.6 | async-start | bytes 6291456 | tf_op jit(solution)/shard_map/all_gather | solution.py:399
  8.0 115.4 %all-gather.7.cloned.1.call-start = ((), (), s32[]{:S(2)}) async-start(), calls=%async_computation.7 | async-start | bytes 4734976 | tf_op jit(solution)/shard_map/all_gather | solution.py:389
  10.5 165.1 %all-gather.11.cloned.1.call-start = ((), (), s32[]{:S(2)}) async-start(), calls=%async_computation.9 | async-start | bytes 2228224 | tf_op jit(solution)/shard_map/all_gather | solution.py:392
  11.3 35.8 %copy-start.11 = (f32[1024,4]{0,1:T(4,128)S(1)}, f32[1024,4]{0,1:T(4,128)}, u32[]{:S(2)}) copy-start(f32[1024,4]{0,1:T(4,128)} %param.25) | copy-start | bytes 49156
  11.3 35.8 %copy-start.12 = (f32[1024]{0:T(1024)S(1)}, f32[1024]{0:T(1024)}, u32[]{:S(2)}) copy-start(f32[1024]{0:T(1024)} %param.26) | copy-start | bytes 12292
  11.3 211.2 %all-gather.9.cloned.1.call-start = ((), (), s32[]{:S(2)}) async-start(), calls=%async_computation.8 | async-start | bytes 6291456 | tf_op jit(solution)/shard_map/all_gather | solution.py:393
  11.9 469.0 %reduce-scatter.11.cloned.1.call-start = ((), (), s32[]{:S(2)}) async-start(), calls=%async_computation.11 | async-start | bytes 15728640 | tf_op jit(solution)/shard_map/reduce_scatter | solution.py:460
  73.7 49.7 %copy-start.19 = (f32[16]{0:T(128)S(1)}, f32[16]{0:T(128)}, u32[]{:S(2)}) copy-start(f32[16]{0:T(128)} %param.29) | copy-start | bytes 196
  126.8 18.0 %copy-start.5 = (f32[2048,16]{0,1:T(8,128)}, f32[2048,16]{0,1:T(8,128)S(1)}, u32[]{:S(2)}) copy-start(f32[2048,16]{0,1:T(8,128)S(1)} %get-tuple-element.133) | copy-start | bytes 393220
  242.7 11.0 %copy-start.4 = (f32[2048,1024]{1,0:T(8,128)S(1)}, f32[2048,1024]{1,0:T(8,128)}, u32[]{:S(2)}) copy-start(f32[2048,1024]{1,0:T(8,128)} %get-tuple-element.31.gated_ref) | copy-start | bytes 25165828
  242.7 11.0 %copy-start.20 = (bf16[1024,1024]{1,0:T(8,128)(2,1)S(1)}, bf16[1024,1024]{1,0:T(8,128)(2,1)}, u32[]{:S(2)}) copy-start(bf16[1024,1024]{1,0:T(8,128)(2,1)} %all-gather.11.cloned.1.call-done) | copy-start | bytes 6291460
  343.6 5.6 copy-start.6
  357.8 189.0 %reduce-scatter.19.cloned.1.call-start = ((), (), s32[]{:S(2)}) async-start(), calls=%async_computation.15 | async-start | bytes 2228224
  361.9 262.4 %reduce-scatter.17.cloned.1.call-start = ((), (), s32[]{:S(2)}) async-start(), calls=%async_computation.14 | async-start | bytes 4734976 | tf_op jit(solution)/shard_map/reduce_scatter | solution.py:459
  380.1 305.2 %reduce-scatter.13.cloned.1.call-start = ((), (), s32[]{:S(2)}) async-start(), calls=%async_computation.12 | async-start | bytes 1392640 | tf_op jit(solution)/shard_map/reduce_scatter | solution.py:485
  490.5 295.6 %reduce-scatter.9.cloned.1.call-start = ((), (), s32[]{:S(2)}) async-start(), calls=%async_computation.10 | async-start | bytes 12582912 | tf_op jit(solution)/shard_map/reduce_scatter | solution.py:438
  491.2 306.9 %reduce-scatter.15.cloned.1.call-start = ((), (), s32[]{:S(2)}) async-start(), calls=%async_computation.13 | async-start | bytes 122880 | tf_op jit(solution)/shard_map/reduce_scatter | solution.py:488
  (10 other events, 24.3 us)
Sparse Core Ops, SparseCore 0:
  9.6 59.4 all-gather.4
  71.4 51.9 all-gather.6
  125.6 39.9 all-gather.10
  166.9 55.5 all-gather.8
  357.9 122.9 reduce-scatter.10
  485.1 61.6 reduce-scatter.18
  551.2 73.0 reduce-scatter.16
  627.9 57.3 reduce-scatter.12
  687.7 98.3 reduce-scatter.8
  788.1 9.9 reduce-scatter.14
